TPU v7x, 32 devices: a whole 2x2x4 slice. The times are simulated.
32 devices in a mesh: wide: 8 (over z, x), narrow: 4 (over y, core).
Axes of the slice: x: 2, y: 2, z: 4, core: 2. Of those that a mesh axis runs over, the one named last changes fastest.
Arguments:
- hidden_in: bfloat16 [32768, 768], P(('wide', 'narrow')), may hold values from -6 to 6
- out_grad: bfloat16 [32768, 768], P(('wide', 'narrow')), may hold values from -6 to 6
- w_qkv: bfloat16 [768, 2304], replicated, may hold values from -0.3125 to 0.3125
- b_query: bfloat16 [768], replicated, may hold values from -3 to 3
- b_value: bfloat16 [768], replicated, may hold values from -3 to 3
- w_out: bfloat16 [768, 768], replicated, may hold values from -1.25 to 1.25
- b_out: bfloat16 [768], replicated, may hold values from -3 to 3
- ln1_gain: bfloat16 [768], replicated, may hold values from 0.25 to 1.75
- ln1_bias: bfloat16 [768], replicated, may hold values from -3 to 3
- w_in: bfloat16 [768, 3072], replicated, may hold values from -0.21875 to 0.21875
- b_in: bfloat16 [3072], replicated, may hold values from -3 to 3
- w_ff_out: bfloat16 [3072, 768], replicated, may hold values from -0.15625 to 0.15625
- b_ff_out: bfloat16 [768], replicated, may hold values from -3 to 3
- ln2_gain: bfloat16 [768], replicated, may hold values from 0.25 to 1.75
- ln2_bias: bfloat16 [768], replicated, may hold values from -3 to 3
- doc_count: int32 [32], replicated, may hold values from 1 to 8, as said below
- single_flag: int32 [32, 8], replicated, may hold values from 0 to 1, as said below
Outputs:
- block_out: bfloat16 [32768, 768], P(('wide', 'narrow'))
- loss: float32 [], replicated
- span_loss: float32 [256], P(('wide', 'narrow'))
- grad_in: float32 [32768, 768], P(('wide', 'narrow'))
- grad_w_qkv: float32 [768, 2304], replicated
- grad_b_query: float32 [768], replicated
- grad_b_value: float32 [768], replicated
- grad_w_out: float32 [768, 768], replicated
- grad_b_out: float32 [768], replicated
- grad_ln1_gain: float32 [768], replicated
- grad_ln1_bias: float32 [768], replicated
- grad_w_in: float32 [768, 3072], replicated
- grad_b_in: float32 [3072], replicated
- grad_w_ff_out: float32 [3072, 768], replicated
- grad_b_ff_out: float32 [768], replicated
- grad_ln2_gain: float32 [768], replicated
- grad_ln2_bias: float32 [768], replicated
Inputs may be any that keep to these rules, and one draw needn't show every extreme that they name: doc_count[d] whole documents stand on device d (mesh index, wide slowest); its k-th document takes 2 - single_flag[d, k] consecutive span slots from slot 0 on, together at most 8; slots after them are empty. In every draw some device holds 8 single-span documents and another holds one document of two spans. `single_flag`: entries at k >= doc_count[d] are not read.
All inputs are finite; a program needn't handle non-finite values.
Results may differ from a plain program's by a relative error of at most 0.014.
The roundings to bfloat16 on the way count: a program that leaves them out, or rounds other values in their place, can miss the bound.
Values may be sent and summed in bfloat16 or wider, within the bound.
A program may use at most 192 MiB of HBM per device.

v0:
```python
import jax
import jax.numpy as jnp
from jax import lax
from jax.sharding import PartitionSpec as P

HEADS = 12
HEAD_DIM = 64
SPAN_LEN = 128


ln_eps = 1e-06
score_scale = 0.2
far_low = -1000000000.0


def combined_all(part, axis, combine):
    gathered = jax.tree.map(lambda a: lax.all_gather(a, axis), part)

    def take(source):
        return jax.tree.map(lambda a: lax.dynamic_index_in_dim(a, source, 0, False), gathered)

    return lax.fori_loop(
        1, lax.axis_size(axis), lambda source, state: combine(state, take(source)), take(0)
    )


def span_layout(doc_count, single_flag):
    slot_total = single_flag.shape[1]
    places = jnp.arange(slot_total, dtype=jnp.int32)
    live_doc = places[None, :] < doc_count[:, None]
    length = jnp.where(live_doc, 2 - single_flag, 0)
    begins = jnp.cumsum(length, axis=1) - length
    inside = (places[None, :, None] >= begins[:, None, :]) & (
        places[None, :, None] < (begins + length)[:, None, :]
    )
    live = jnp.any(inside, axis=2)
    double = inside & (length[:, None, :] == 2)
    has_pair = jnp.any(double, axis=2)
    other = jnp.sum(
        jnp.where(double, 2 * begins[:, None, :] + 1 - places[None, :, None], 0), axis=2
    )
    other = jnp.where(has_pair, other, places[None, :])
    offsets = jnp.arange(single_flag.shape[0], dtype=jnp.int32) * slot_total
    return (live, has_pair, offsets[:, None] + other)


def matmul(left, right):
    return jnp.dot(left, right, preferred_element_type=jnp.float32)


def matmul_left_t(left, right):
    return lax.dot_general(
        left, right, (((0,), (0,)), ((), ())), preferred_element_type=jnp.float32
    )


def matmul_right_t(left, right):
    return lax.dot_general(
        left, right, (((1,), (1,)), ((), ())), preferred_element_type=jnp.float32
    )


def split_heads(block, span_count):
    return block.reshape(span_count, SPAN_LEN, HEADS, HEAD_DIM)


def head_scores(queries, keys_low):
    return jnp.einsum(
        "slhe,smhe->shlm", queries, keys_low, preferred_element_type=jnp.float32
    ) * HEAD_DIM ** (-0.5)


def layer_norm_parts(values, gain, shift):
    centered = values - jnp.mean(values, axis=1, keepdims=True)
    scale = lax.rsqrt(jnp.mean(centered * centered, axis=1, keepdims=True) + ln_eps)
    normed = centered * scale
    return (normed * gain + shift, normed, scale)


def norm_back(upstream, normed, scale, gain):
    scaled = upstream * gain
    return scale * (
        scaled
        - jnp.mean(scaled, axis=1, keepdims=True)
        - normed * jnp.mean(scaled * normed, axis=1, keepdims=True)
    )


def exact_gelu(values):
    return jax.nn.gelu(values, approximate=False)


def stats_combine(earlier, later):
    new_top = jnp.maximum(earlier[0], later[0])
    return (
        new_top,
        earlier[1] * jnp.exp(earlier[0] - new_top) + later[1] * jnp.exp(later[0] - new_top),
    )


def row_block(table, wide_at, n_wide, n_narrow):
    shaped = table.reshape(n_wide, n_narrow, -1)
    return lax.dynamic_index_in_dim(shaped, wide_at, 0, keepdims=False).reshape(-1)


def col_block(table, narrow_at, n_wide, n_narrow):
    shaped = table.reshape(n_wide, n_narrow, -1)
    return lax.dynamic_index_in_dim(shaped, narrow_at, 1, keepdims=False).reshape(-1)


def per_device(
    hidden_in,
    out_grad,
    w_qkv,
    b_query,
    b_value,
    w_out,
    b_out,
    ln1_gain,
    ln1_bias,
    w_in,
    b_in,
    w_ff_out,
    b_ff_out,
    ln2_gain,
    ln2_bias,
    doc_count,
    single_flag,
):
    row_count, model_width = hidden_in.shape
    span_count = row_count // SPAN_LEN
    head_scale = HEAD_DIM ** (-0.5)
    inputs = hidden_in.astype(jnp.float32)
    gain_one = ln1_gain.astype(jnp.float32)
    gain_two = ln2_gain.astype(jnp.float32)
    packed = matmul(hidden_in, w_qkv)
    queries = split_heads(
        (packed[:, :model_width] + b_query.astype(jnp.float32)).astype(jnp.bfloat16), span_count
    )
    keys_low = split_heads(
        packed[:, model_width : 2 * model_width].astype(jnp.bfloat16), span_count
    )
    values_low = split_heads(
        (packed[:, 2 * model_width :] + b_value.astype(jnp.float32)).astype(jnp.bfloat16),
        span_count,
    )
    scores = head_scores(queries, keys_low)
    score_top = jnp.max(scores, axis=3, keepdims=True)
    shifted = jnp.exp(scores - score_top)
    score_total = jnp.sum(shifted, axis=3, keepdims=True)
    log_total = score_top + jnp.log(score_total)
    probs_low = (shifted / score_total).astype(jnp.bfloat16)
    context = jnp.einsum(
        "shlm,smhe->slhe", probs_low, values_low, preferred_element_type=jnp.float32
    )
    context = context.reshape(row_count, model_width).astype(jnp.bfloat16)
    attended = matmul(context, w_out) + b_out.astype(jnp.float32)
    mixed, normed_one, scale_one = layer_norm_parts(
        inputs + attended, gain_one, ln1_bias.astype(jnp.float32)
    )
    mixed_low = mixed.astype(jnp.bfloat16)
    hidden = matmul(mixed_low, w_in) + b_in.astype(jnp.float32)
    activation, gelu_back = jax.vjp(exact_gelu, hidden)
    act_low = activation.astype(jnp.bfloat16)
    ffn = matmul(act_low, w_ff_out) + b_ff_out.astype(jnp.float32)
    block_float, normed_two, scale_two = layer_norm_parts(
        mixed + ffn, gain_two, ln2_bias.astype(jnp.float32)
    )
    block_out = block_float.astype(jnp.bfloat16)
    cls_low = block_out.reshape(span_count, SPAN_LEN, model_width)[:, 0, :]
    row_cls = lax.all_gather(cls_low, "narrow", axis=0, tiled=True)
    col_cls = lax.all_gather(cls_low, "wide", axis=0, tiled=True)
    n_wide = lax.axis_size("wide")
    n_narrow = lax.axis_size("narrow")
    wide_at = lax.axis_index("wide")
    narrow_at = lax.axis_index("narrow")
    live, has_pair, mate = span_layout(doc_count, single_flag)
    span_ids = jnp.arange(n_wide * n_narrow * span_count, dtype=jnp.int32)
    row_ids = row_block(span_ids, wide_at, n_wide, n_narrow)
    row_pair = row_block(has_pair, wide_at, n_wide, n_narrow)
    row_mate = row_block(mate, wide_at, n_wide, n_narrow)
    col_ids = col_block(span_ids, narrow_at, n_wide, n_narrow)
    col_live = col_block(live, narrow_at, n_wide, n_narrow)
    sims = score_scale * matmul_right_t(row_cls, col_cls)
    allowed = col_live[None, :] & (col_ids[None, :] != row_ids[:, None])
    masked = jnp.where(allowed, sims, far_low)
    part_top = jnp.max(masked, axis=1)
    part_total = jnp.sum(jnp.exp(masked - part_top[:, None]), axis=1)
    row_top, row_total = combined_all((part_top, part_total), "narrow", stats_combine)
    row_lse = row_top + jnp.log(row_total)
    matches = col_ids[None, :] == row_mate[:, None]
    positive = jnp.sum(jnp.where(matches, sims, 0.0), axis=1)
    row_loss = jnp.where(row_pair, row_lse - positive, 0.0)
    span_loss = lax.dynamic_slice_in_dim(row_loss, narrow_at * span_count, span_count)
    loss_part = jnp.sum(span_loss)
    sim_probs = jnp.exp(masked - row_lse[:, None])
    sim_grad = jnp.where(row_pair[:, None], sim_probs - matches.astype(jnp.float32), 0.0).astype(
        jnp.bfloat16
    )
    cls_grad = lax.psum_scatter(
        (score_scale * matmul(sim_grad, col_cls)).astype(jnp.bfloat16),
        "narrow",
        scatter_dimension=0,
        tiled=True,
    ).astype(jnp.float32)
    cls_grad = cls_grad + lax.psum_scatter(
        (score_scale * matmul_left_t(sim_grad, row_cls)).astype(jnp.bfloat16),
        "wide",
        scatter_dimension=0,
        tiled=True,
    ).astype(jnp.float32)
    upper_grad = out_grad.astype(jnp.float32).reshape(span_count, SPAN_LEN, model_width)
    top_grad = jnp.concatenate([cls_grad[:, None, :], upper_grad[:, 1:, :]], axis=1).reshape(
        row_count, model_width
    )
    grad_ln2_gain = jnp.sum(top_grad * normed_two, axis=0)
    grad_ln2_bias = jnp.sum(top_grad, axis=0)
    pre_two_grad = norm_back(top_grad, normed_two, scale_two, gain_two)
    ffn_grad = pre_two_grad.astype(jnp.bfloat16)
    grad_b_ff_out = jnp.sum(ffn_grad.astype(jnp.float32), axis=0)
    grad_w_ff_out = matmul_left_t(act_low, ffn_grad)
    hidden_grad = gelu_back(matmul_right_t(ffn_grad, w_ff_out))[0].astype(jnp.bfloat16)
    grad_b_in = jnp.sum(hidden_grad.astype(jnp.float32), axis=0)
    grad_w_in = matmul_left_t(mixed_low, hidden_grad)
    mixed_grad = pre_two_grad + matmul_right_t(hidden_grad, w_in)
    grad_ln1_gain = jnp.sum(mixed_grad * normed_one, axis=0)
    grad_ln1_bias = jnp.sum(mixed_grad, axis=0)
    pre_one_grad = norm_back(mixed_grad, normed_one, scale_one, gain_one)
    attn_grad = pre_one_grad.astype(jnp.bfloat16)
    grad_b_out = jnp.sum(attn_grad.astype(jnp.float32), axis=0)
    grad_w_out = matmul_left_t(context, attn_grad)
    context_grad = split_heads(matmul_right_t(attn_grad, w_out).astype(jnp.bfloat16), span_count)
    probs_again = jnp.exp(head_scores(queries, keys_low) - log_total)
    probs_again_low = probs_again.astype(jnp.bfloat16)
    value_grad = jnp.einsum(
        "shlm,slhe->smhe", probs_again_low, context_grad, preferred_element_type=jnp.float32
    ).astype(jnp.bfloat16)
    prob_grad = jnp.einsum(
        "slhe,smhe->shlm", context_grad, values_low, preferred_element_type=jnp.float32
    )
    score_grad = (
        probs_again * (prob_grad - jnp.sum(probs_again * prob_grad, axis=3, keepdims=True))
    ).astype(jnp.bfloat16)
    query_grad = (
        jnp.einsum("shlm,smhe->slhe", score_grad, keys_low, preferred_element_type=jnp.float32)
        * head_scale
    ).astype(jnp.bfloat16)
    key_grad = (
        jnp.einsum("shlm,slhe->smhe", score_grad, queries, preferred_element_type=jnp.float32)
        * head_scale
    ).astype(jnp.bfloat16)
    query_grad = query_grad.reshape(row_count, model_width)
    key_grad = key_grad.reshape(row_count, model_width)
    value_grad = value_grad.reshape(row_count, model_width)
    packed_grad = jnp.concatenate([query_grad, key_grad, value_grad], axis=1)
    grad_b_query = jnp.sum(query_grad.astype(jnp.float32), axis=0)
    grad_b_value = jnp.sum(value_grad.astype(jnp.float32), axis=0)
    grad_w_qkv = matmul_left_t(hidden_in, packed_grad)
    grad_in = pre_one_grad + matmul_right_t(packed_grad, w_qkv)
    (
        grad_w_qkv,
        grad_b_query,
        grad_b_value,
        grad_w_out,
        grad_b_out,
        grad_ln1_gain,
        grad_ln1_bias,
        grad_w_in,
        grad_b_in,
        grad_w_ff_out,
        grad_b_ff_out,
        grad_ln2_gain,
        grad_ln2_bias,
        loss_part,
    ) = lax.psum(
        (
            grad_w_qkv,
            grad_b_query,
            grad_b_value,
            grad_w_out,
            grad_b_out,
            grad_ln1_gain,
            grad_ln1_bias,
            grad_w_in,
            grad_b_in,
            grad_w_ff_out,
            grad_b_ff_out,
            grad_ln2_gain,
            grad_ln2_bias,
            loss_part,
        ),
        ("wide", "narrow"),
    )
    return (
        block_out,
        loss_part,
        span_loss,
        grad_in,
        grad_w_qkv,
        grad_b_query,
        grad_b_value,
        grad_w_out,
        grad_b_out,
        grad_ln1_gain,
        grad_ln1_bias,
        grad_w_in,
        grad_b_in,
        grad_w_ff_out,
        grad_b_ff_out,
        grad_ln2_gain,
        grad_ln2_bias,
    )


def solution(mesh):
    placed = (
        P(("wide", "narrow"), None),
        P(("wide", "narrow"), None),
        P(),
        P(),
        P(),
        P(),
        P(),
        P(),
        P(),
        P(),
        P(),
        P(),
        P(),
        P(),
        P(),
        P(),
        P(),
    )
    return jax.shard_map(
        per_device,
        mesh=mesh,
        in_specs=placed,
        out_specs=(
            P(("wide", "narrow"), None),
            P(),
            P(("wide", "narrow")),
            P(("wide", "narrow"), None),
            P(),
            P(),
            P(),
            P(),
            P(),
            P(),
            P(),
            P(),
            P(),
            P(),
            P(),
            P(),
            P(),
        ),
        check_vma=False,
    )
```

profile of v0, /device:TPU:0, one launch (start us, length us, event | category | flops | bytes accessed | tf_op | source)
XLA Modules:
  0.0 830.4 jit_solution(15169349308725948530)
XLA Ops:
  17.0 5.2 fusion.80
  23.5 2.3 fusion.13
  25.8 2.8 copy.133
  28.7 3.0 copy.164
  31.7 2.6 copy.135
  34.3 3.0 copy.166
  37.4 2.6 copy.134
  39.9 2.0 copy.165
  41.9 1.3 multiply_reduce_fusion.1
  43.3 1.7 fusion.8
  46.0 1.4 fusion.26
  49.2 1.7 fusion.78
  51.6 1.9 copy-done.26
  53.5 35.6 %multiply_convert_fusion = (bf16[1024,3072]{1,0:T(8,128)(2,1)S(1)}, f32[1024,3072]{1,0:T(8,128)}, f32[1024,3072]{1,0:T(8,128)}) fusion(f32[3072]{0:T(1024)S(1)} %copy-done.31, bf16[768,3072]{1,0:T(8,128)(2,1)S(1)} %bitcast.160, f32[1024,768]{1,0:T(8,128)S(1)} %get-tuple-element.298, f32[768]{0:T(1024)S(1)} %copy-done.26, ...), kind=kOutput, calls=%fused_computation.10 | convolution fusion | flops 5043388416 | bytes 39348224 | tf_op jit(solution)/shard_map/dot_general | solution.py:48
  89.1 5.4 fusion.79
  97.5 6.6 all-gather
  104.1 33.3 %all-gather.1 = bf16[64,1,768]{2,0,1:T(8,128)(2,1)} all-gather(bf16[8,1,768]{2,0,1:T(8,128)(2,1)S(1)} %copy.163), channel_id=3, replica_groups=mesh['wide'=8,'narrow'=4] {'wide'}, dimensions={0}, use_global_device_ids=true | all-gather | bytes 110592 | tf_op jit(solution)/shard_map/all_gather | solution.py:172
  140.7 1.3 fusion.52
  142.0 1.3 select_reduce_fusion
  143.3 1.3 copy.142
  146.0 1.3 and.26
  152.2 1.4 copy.144
  153.6 1.3 dynamic-slice_reduce_fusion.1
  156.2 1.4 fusion.62
  162.0 2.3 fusion.61
  166.1 1.5 fusion.57
  169.3 6.3 all-reduce.4
  176.9 1.3 reshape.228
  178.2 3.9 while.17
  178.2 1.3 fusion.100
  179.5 1.3 fusion.100
  183.9 1.8 fusion.45
  185.8 1.8 fusion.44
  187.9 3.5 slice_convert_fusion.1
  192.0 14.4 %reduce-scatter.3.cloned.1.call-done = bf16[8,768]{1,0:T(8,128)(2,1)} async-done(((bf16[32,768]{1,0:T(8,128)(2,1)}), bf16[8,768]{1,0:T(8,128)(2,1)}) %reduce-scatter.3.cloned.1.call-update) | async-done | bytes 12304 | tf_op jit(solution)/shard_map/reduce_scatter | solution.py:200
  206.4 61.3 %reduce-scatter.5.cloned.1.call-done = bf16[8,768]{1,0:T(8,128)(2,1)} async-done(((bf16[64,768]{1,0:T(8,128)(2,1)}), bf16[8,768]{1,0:T(8,128)(2,1)}) %reduce-scatter.5.cloned.1.call-update) | async-done | bytes 12304 | tf_op jit(solution)/shard_map/reduce_scatter | solution.py:206
  267.6 1.3 fusion.54
  269.0 2.5 multiply_reduce_fusion.5
  271.8 1.5 fusion.14
  273.4 1.9 convert_reduce_fusion.1
  275.3 7.8 fusion.65
  283.1 19.5 %convert_reduce_fusion = (f32[3072]{0:T(1024)}, bf16[1024,3072]{1,0:T(8,128)(2,1)}) fusion(f32[1024,3072]{1,0:T(8,128)} %get-tuple-element.290, bf16[3072,768]{1,0:T(8,128)(2,1)} %param.30, f32[1024,768]{1,0:T(8,128)} %copy-done.14, f32[1024,3072]{1,0:T(8,128)} %get-tuple-element.299, f32[3072]{0:T(1024)S(1)} %copy-done.32), kind=kOutput, calls=%fused_computation.8 | convolution fusion | flops 4886098944 | bytes 39346176 | tf_op jit(solution)/shard_map/dot_general | solution.py:58
  302.6 11.6 %multiply_reduce_fusion.2 = (f32[768]{0:T(1024)}, f32[1024]{0:T(1024)S(1)}, f32[1024]{0:T(1024)S(1)}, f32[768]{0:T(1024)}, f32[1024,768]{1,0:T(8,128)S(1)}) fusion(f32[1024,768]{1,0:T(8,128)} %copy-done.4, f32[1024]{0:T(1024)S(1)} %add_rsqrt_fusion.1, f32[1024]{0:T(1024)S(1)} %broadcast_multiply_fusion.4, f32[768]{0:T(1024)S(1)} %convert_element_type.140, ...), kind=kOutput, calls=%fused_computation.44 | convolution fusion | flops 4839698432 | bytes 20472832 | tf_op jit(solution)/shard_map/dot_general | solution.py:58
  314.2 8.7 %fusion.72 = f32[768,3072]{1,0:T(8,128)} fusion(bf16[1024,3072]{1,0:T(8,128)(2,1)S(1)} %copy-done.10, f32[1024,768]{1,0:T(8,128)S(1)} %copy-done.5, f32[768]{0:T(1024)S(1)} %copy-done.27, f32[768]{0:T(1024)S(1)} %convert_element_type.140, f32[1024]{0:T(1024)S(1)} %add_rsqrt_fusion.1, f32[1024]{0:T(1024)S(1)} %broadcast_multiply_fusion.4), kind=kOutput, calls=%fused_computation.156 | convolution fusion | flops 4835770368 | bytes 18888704 | tf_op jit(solution)/shard_map/dot_general | solution.py:52
  322.9 1.7 convert_reduce_fusion.2
  324.6 2.8 fusion.23
  327.4 2.6 convolution_convert_fusion
  330.0 2.6 copy.146
  332.6 1.9 copy.168
  334.5 5.3 convert_reduce_fusion.3
  339.8 6.2 multiply_reduce_fusion
  346.0 4.9 multiply_convert_fusion.1
  351.0 2.3 fusion.28
  359.2 2.3 copy-done.21
  361.5 5.8 convolution_bitcast_fusion
  367.3 1.8 fusion.76
  369.2 2.5 fusion.46
  373.1 43.9 %all-reduce.2 = (f32[]{:T(128)}, f32[768]{0:T(1024)}, f32[768]{0:T(1024)}, f32[768]{0:T(1024)}, f32[768]{0:T(1024)}, /*index=5*/f32[768]{0:T(1024)}, f32[3072]{0...) all-reduce(f32[]{:T(128)} %get-tuple-element.281, ...), channel_id=1, replica_groups=mesh['wide'=8,'narrow'=4] {'wide','narrow'}, use_global_device_ids=true, to_apply=%region_16.17 | all-reduce | flops 9217 | bytes 73736 | tf_op jit(solution)/shard_map/psum | solution.py:275
  417.0 8.5 %convolution_add_fusion.1 = f32[1024,768]{1,0:T(8,128)} fusion(f32[1024,768]{1,0:T(8,128)} %copy-done.13, bf16[1024,2304]{0,1:T(8,128)(2,1)} %copy-done.21, bf16[768,2304]{1,0:T(8,128)(2,1)S(1)} %copy-done), kind=kOutput, calls=%fused_computation.69 | convolution fusion | flops 3624665088 | bytes 14548992 | tf_op jit(solution)/shard_map/dot_general | solution.py:58
  425.5 374.3 %all-reduce.7.cloned.1.call-done = (f32[768,2304]{0,1:T(8,128)}, f32[768,768]{1,0:T(8,128)}, f32[768,3072]{1,0:T(8,128)}, f32[3072,768]{1,0:T(8,128)}) async-done(((f32[768,2304]{0,1:T(8,128)}, f32[768,768]{1,0:T(8,128)}, f32[768,3072]{1,0:T(8,128)}, f32[3072,768]{1,0:T(8,128)}), (f32[768,2304]{0,1:T(8,128)}, f32[768,768]{1,0:T(8,128)}, f32[768,3072]{1,0:T(8,128)}, ...) | async-done | bytes 28311568 | tf_op jit(solution)/shard_map/psum | solution.py:275
  799.8 8.0 copy.158
  807.8 3.4 copy.230
  811.1 8.8 %copy.231 = f32[768,3072]{1,0:T(8,128)} copy(f32[768,3072]{1,0:T(8,128)} %get-tuple-element.385) | data formatting | bytes 18874368
  819.9 3.7 copy.232
  (168 shorter events, 48.5 us)
Async XLA Ops:
  7.2 9.8 %copy-start = (bf16[768,2304]{1,0:T(8,128)(2,1)S(1)}, bf16[768,2304]{1,0:T(8,128)(2,1)}, u32[]{:S(2)}) copy-start(bf16[768,2304]{1,0:T(8,128)(2,1)} %param.21) | copy-start | bytes 10616836
  7.2 199.2 %reduce-scatter.3.cloned.1.call-start = ((), (), s32[]{:S(2)}) async-start(), calls=%async_computation.2 | async-start | bytes 61440 | tf_op jit(solution)/shard_map/reduce_scatter | solution.py:200
  39.9 2.0 copy-start.6
  41.9 1.3 copy-start.8
  43.3 2.7 copy-start.1
  43.3 2.7 copy-start.19
  43.3 2.7 copy-start.11
  45.0 2.4 copy-start.22
  47.4 1.4 copy-start.35
  47.4 1.7 copy-start.37
  48.7 2.2 copy-start.16
  48.7 2.9 slice-start.7
  49.2 2.4 slice-start.8
  49.2 39.9 %slice-start.5 = ((s8[4718592]{0:T(1024)(128)(4,1)}), s8[4194304]{0:T(1024)(128)(4,1)S(1)}, s32[]{:S(2)}) async-start(s8[4718592]{0:T(1024)(128)(4,1)} %bitcast.157), calls=%async_computation.10 | async-start | bytes 8388608
  50.9 38.2 %copy-start.4 = (f32[1024,768]{1,0:T(8,128)}, f32[1024,768]{1,0:T(8,128)S(1)}, u32[]{:S(2)}) copy-start(f32[1024,768]{1,0:T(8,128)S(1)} %get-tuple-element.298) | copy-start | bytes 9437188
  50.9 2.6 copy-start.26
  50.9 2.6 copy-start.31
  53.5 35.6 %copy-start.33 = (f32[768]{0:T(1024)S(1)}, f32[768]{0:T(1024)}, u32[]{:S(2)}) copy-start(f32[768]{0:T(1024)} %convert_element_type.145) | copy-start | bytes 9220
  53.5 35.6 %slice-start.6 = ((s8[4718592]{0:T(1024)(128)(4,1)}), s8[524288]{0:T(1024)(128)(4,1)S(1)}, s32[]{:S(2)}) async-start(s8[4718592]{0:T(1024)(128)(4,1)} %bitcast.157), calls=%async_computation.11 | async-start | bytes 1048576
  89.1 5.5 copy-start.39
  94.6 1.8 copy-start.2
  94.6 0.7 copy-start.30
  94.6 1.7 copy-start.24
  95.3 2.2 copy-start.28
  96.3 1.1 copy-start.15
  183.4 0.5 copy-start.34
  185.7 81.9 %reduce-scatter.5.cloned.1.call-start = ((), (), s32[]{:S(2)}) async-start(), calls=%async_computation.3 | async-start | bytes 110592 | tf_op jit(solution)/shard_map/reduce_scatter | solution.py:206
  187.6 612.2 %all-reduce.7.cloned.1.call-start = ((), (), s32[]{:S(2)}) async-start(), calls=%async_computation.4 | async-start | bytes 56623104 | tf_op jit(solution)/shard_map/psum | solution.py:275
  187.8 3.5 copy-start.20
  187.8 3.5 copy-start.23
  269.0 2.8 copy-start.3
  269.0 2.8 copy-start.25
  269.0 2.8 copy-start.29
  271.8 3.5 slice-start.9
  273.4 1.9 slice-start.10
  275.3 7.8 copy-start.14
  275.3 7.8 copy-start.32
  302.6 11.6 %copy-start.5 = (f32[1024,768]{1,0:T(8,128)S(1)}, f32[1024,768]{1,0:T(8,128)}, u32[]{:S(2)}) copy-start(f32[1024,768]{1,0:T(8,128)} %copy-done.4) | copy-start | bytes 9437188
  302.6 11.6 %copy-start.10 = (bf16[1024,3072]{1,0:T(8,128)(2,1)S(1)}, bf16[1024,3072]{1,0:T(8,128)(2,1)}, u32[]{:S(2)}) copy-start(bf16[1024,3072]{1,0:T(8,128)(2,1)} %get-tuple-element.312) | copy-start | bytes 18874372
  302.6 11.6 %copy-start.27 = (f32[768]{0:T(1024)S(1)}, f32[768]{0:T(1024)}, u32[]{:S(2)}) copy-start(f32[768]{0:T(1024)} %convert_element_type.141) | copy-start | bytes 9220
  322.9 1.7 copy-start.17
  324.6 2.8 copy-start.13
  324.6 2.8 copy-start.38
  332.6 1.9 copy-start.18
  334.5 5.3 copy-start.12
  334.5 11.5 %slice-start = ((s8[6291456]{0:T(1024)(128)(4,1)}), s8[4194304]{0:T(1024)(128)(4,1)S(1)}, s32[]{:S(2)}) async-start(s8[6291456]{0:T(1024)(128)(4,1)} %bitcast.127), calls=%async_computation.5 | async-start | bytes 8388608
  339.8 6.2 slice-start.1
  346.0 4.9 copy-start.9
  351.0 2.3 copy-start.7
  358.4 3.1 copy-start.36
  359.2 2.3 copy-start.21
  807.8 12.1 %slice-start.2 = ((s8[9437184]{0:T(1024)(128)(4,1)}), s8[4194304]{0:T(1024)(128)(4,1)S(1)}, s32[]{:S(2)}) async-start(s8[9437184]{0:T(1024)(128)(4,1)} %bitcast.135), calls=%async_computation.7 | async-start | bytes 8388608
  811.1 8.8 %slice-start.3 = ((s8[9437184]{0:T(1024)(128)(4,1)}), s8[4194304]{0:T(1024)(128)(4,1)S(1)}, s32[]{:S(2)}) async-start(s8[9437184]{0:T(1024)(128)(4,1)} %bitcast.135), calls=%async_computation.8 | async-start | bytes 8388608
  811.1 8.8 %slice-start.4 = ((s8[9437184]{0:T(1024)(128)(4,1)}), s8[1048576]{0:T(1024)(128)(4,1)S(1)}, s32[]{:S(2)}) async-start(s8[9437184]{0:T(1024)(128)(4,1)} %bitcast.135), calls=%async_computation.9 | async-start | bytes 2097152
Sparse Core Ops, SparseCore 0:
  185.8 20.4 reduce-scatter.2
  210.0 57.6 reduce-scatter.4
  367.5 432.2 all-reduce.6
where the time goes:
time: 835 us; the launch traced here: 830 us
  waiting for transfers between devices  450 us (54%)
  matrix products  139 us (17%)
  blocking collectives  90.1 us (11%)
  local copies, waits for them, and re-layouts  83.7 us (10%)
  other arithmetic  52.3 us (6%)
  between operations  15.2 us (2%)
    psum x1, waiting for transfers between devices, per_device(): lax.psum((grad_w_qkv, grad_b_query, grad_b_value, grad_w_out, grad_b_out,...  374 us
    reduce_scatter x1, waiting for transfers between devices, per_device(): lax.psum_scatter((score_scale * matmul_left_t(sim_grad, row_cls)).astype(...  61.3 us
    dot_general x5, matrix products, matmul(): return jnp.dot(left, right, preferred_element_type=jnp.float32)  49.7 us
    unnamed x118, local copies, waits for them, and re-layouts  47.8 us
    dot_general x5, matrix products, matmul_right_t(): lax.dot_general(left, right, (((1,), (1,)), ((), ())), preferred_element_...  44.4 us
    psum x1, blocking collectives, per_device(): lax.psum((grad_w_qkv, grad_b_query, grad_b_value, grad_w_out, grad_b_out,...  43.9 us
    all_gather x1, blocking collectives, per_device(): col_cls = lax.all_gather(cls_low, 'wide', axis=0, tiled=True)  33.3 us
    dot_general x5, matrix products, matmul_left_t(): lax.dot_general(left, right, (((0,), (0,)), ((), ())), preferred_element_...  26.9 us
  transfers between devices with their start and end apart: 3, of which 3 were waited for; matrix products, arithmetic and copies ran while one was open for 2% of the time, Pallas kernels for 0%

commit v1 on v0

--- a/solution.py
+++ b/solution.py
@@ -1,6 +1,10 @@
+import functools
+
 import jax
 import jax.numpy as jnp
 from jax import lax
+from jax.experimental import pallas as pl
+from jax.experimental.pallas import tpu as pltpu
 from jax.sharding import PartitionSpec as P
 
 HEADS = 12
@@ -11,37 +15,6 @@
 ln_eps = 1e-06
 score_scale = 0.2
 far_low = -1000000000.0
-
-
-def combined_all(part, axis, combine):
-    gathered = jax.tree.map(lambda a: lax.all_gather(a, axis), part)
-
-    def take(source):
-        return jax.tree.map(lambda a: lax.dynamic_index_in_dim(a, source, 0, False), gathered)
-
-    return lax.fori_loop(
-        1, lax.axis_size(axis), lambda source, state: combine(state, take(source)), take(0)
-    )
-
-
-def span_layout(doc_count, single_flag):
-    slot_total = single_flag.shape[1]
-    places = jnp.arange(slot_total, dtype=jnp.int32)
-    live_doc = places[None, :] < doc_count[:, None]
-    length = jnp.where(live_doc, 2 - single_flag, 0)
-    begins = jnp.cumsum(length, axis=1) - length
-    inside = (places[None, :, None] >= begins[:, None, :]) & (
-        places[None, :, None] < (begins + length)[:, None, :]
-    )
-    live = jnp.any(inside, axis=2)
-    double = inside & (length[:, None, :] == 2)
-    has_pair = jnp.any(double, axis=2)
-    other = jnp.sum(
-        jnp.where(double, 2 * begins[:, None, :] + 1 - places[None, :, None], 0), axis=2
-    )
-    other = jnp.where(has_pair, other, places[None, :])
-    offsets = jnp.arange(single_flag.shape[0], dtype=jnp.int32) * slot_total
-    return (live, has_pair, offsets[:, None] + other)
 
 
 def matmul(left, right):
@@ -90,22 +63,106 @@
     return jax.nn.gelu(values, approximate=False)
 
 
-def stats_combine(earlier, later):
-    new_top = jnp.maximum(earlier[0], later[0])
-    return (
-        new_top,
-        earlier[1] * jnp.exp(earlier[0] - new_top) + later[1] * jnp.exp(later[0] - new_top),
-    )
-
-
-def row_block(table, wide_at, n_wide, n_narrow):
-    shaped = table.reshape(n_wide, n_narrow, -1)
-    return lax.dynamic_index_in_dim(shaped, wide_at, 0, keepdims=False).reshape(-1)
-
-
-def col_block(table, narrow_at, n_wide, n_narrow):
-    shaped = table.reshape(n_wide, n_narrow, -1)
-    return lax.dynamic_index_in_dim(shaped, narrow_at, 1, keepdims=False).reshape(-1)
+def contrast_kernel(own_ref, cls_ref, count_ref, flag_ref, grad_ref, own_loss_ref, loss_ref):
+    total, width = cls_ref.shape
+    docsets, slots = flag_ref.shape
+    span_count = grad_ref.shape[0]
+    first = own_ref[0] * span_count
+    block = min(total, 256)
+    f32, bf16, i32 = jnp.float32, jnp.bfloat16, jnp.int32
+
+    def layout(at):
+        slot = at + lax.broadcasted_iota(i32, (block, 1), 0)
+        device = slot // slots
+        place = (slot - device * slots).astype(f32)
+        member = lax.broadcasted_iota(i32, (block, docsets), 1) == device
+        count = jnp.sum(jnp.where(member, count_ref[...].astype(f32), 0.0), axis=1, keepdims=True)
+        flags = jnp.dot(
+            member.astype(bf16), flag_ref[...].astype(bf16), preferred_element_type=f32
+        )
+        doc = lax.broadcasted_iota(i32, (block, slots), 1).astype(f32)
+        length = jnp.where(doc < count, 2.0 - flags, 0.0)
+        earlier = lax.broadcasted_iota(i32, (slots, slots), 0) < lax.broadcasted_iota(
+            i32, (slots, slots), 1
+        )
+        begins = jnp.dot(length.astype(bf16), earlier.astype(bf16), preferred_element_type=f32)
+        inside = (place >= begins) & (place < begins + length)
+        double = inside & (length == 2.0)
+        live = jnp.max(inside.astype(f32), axis=1, keepdims=True)
+        pair = jnp.max(double.astype(f32), axis=1, keepdims=True)
+        other = jnp.sum(jnp.where(double, 2.0 * begins + 1.0 - place, 0.0), axis=1, keepdims=True)
+        mate = jnp.where(pair > 0.0, device * slots + other.astype(i32), slot)
+        return slot, live, pair, mate
+
+    eye = lax.broadcasted_iota(i32, (block, block), 0) == lax.broadcasted_iota(
+        i32, (block, block), 1
+    )
+    live_row = jnp.concatenate(
+        [
+            jnp.sum(jnp.where(eye, layout(at)[1], 0.0), axis=0, keepdims=True)
+            for at in range(0, total, block)
+        ],
+        axis=1,
+    )
+    column = lax.broadcasted_iota(i32, (block, total), 1)
+    pick_col = (
+        lax.broadcasted_iota(i32, (span_count, total), 1)
+        == first + lax.broadcasted_iota(i32, (span_count, total), 0)
+    ).astype(bf16)
+    rows_own = jnp.zeros((span_count, total), f32)
+    upward = jnp.zeros((span_count, width), f32)
+    own_loss = jnp.zeros((1, span_count), f32)
+    loss = jnp.zeros((1, 1), f32)
+    for at in range(0, total, block):
+        slot, live, pair, mate = layout(at)
+        cls_block = cls_ref[at : at + block, :]
+        sims = score_scale * lax.dot_general(
+            cls_block, cls_ref[...], (((1,), (1,)), ((), ())), preferred_element_type=f32
+        )
+        allowed = (live_row > 0.0) & (column != slot)
+        masked = jnp.where(allowed, sims, far_low)
+        top = jnp.max(masked, axis=1, keepdims=True)
+        lse = top + jnp.log(jnp.sum(jnp.exp(masked - top), axis=1, keepdims=True))
+        matches = column == mate
+        positive = jnp.sum(jnp.where(matches, sims, 0.0), axis=1, keepdims=True)
+        span_loss = jnp.where(pair > 0.0, lse - positive, 0.0)
+        loss = loss + jnp.sum(span_loss, axis=0, keepdims=True)
+        mine = slot == first + lax.broadcasted_iota(i32, (block, span_count), 1)
+        own_loss = own_loss + jnp.sum(jnp.where(mine, span_loss, 0.0), axis=0, keepdims=True)
+        sim_grad = jnp.where(
+            pair > 0.0, jnp.exp(masked - lse) - matches.astype(f32), 0.0
+        ).astype(bf16)
+        pick_row = (
+            at + lax.broadcasted_iota(i32, (span_count, block), 1)
+            == first + lax.broadcasted_iota(i32, (span_count, block), 0)
+        ).astype(bf16)
+        rows_own = rows_own + jnp.dot(pick_row, sim_grad, preferred_element_type=f32)
+        cols_own = lax.dot_general(
+            pick_col, sim_grad, (((1,), (1,)), ((), ())), preferred_element_type=f32
+        )
+        upward = upward + jnp.dot(cols_own.astype(bf16), cls_block, preferred_element_type=f32)
+    upward = upward + jnp.dot(rows_own.astype(bf16), cls_ref[...], preferred_element_type=f32)
+    grad_ref[...] = score_scale * upward
+    own_loss_ref[...] = own_loss
+    loss_ref[...] = loss
+
+
+def contrast(cls_all, doc_count, single_flag, own, span_count):
+    total, width = cls_all.shape
+    vmem = pl.BlockSpec(memory_space=pltpu.VMEM)
+    cls_grad, own_loss, loss = pl.pallas_call(
+        contrast_kernel,
+        out_shape=(
+            jax.ShapeDtypeStruct((span_count, width), jnp.float32),
+            jax.ShapeDtypeStruct((1, span_count), jnp.float32),
+            jax.ShapeDtypeStruct((1, 1), jnp.float32),
+        ),
+        in_specs=[pl.BlockSpec(memory_space=pltpu.SMEM), vmem, vmem, vmem],
+        out_specs=(vmem, vmem, vmem),
+        compiler_params=pltpu.CompilerParams(vmem_limit_bytes=48 * 1024 * 1024),
+        name="contrast",
+    )(own.reshape(1), cls_all, doc_count.reshape(1, -1), single_flag)
+    return cls_grad, own_loss.reshape(-1), loss.reshape(())
 
 
 def per_device(
@@ -168,47 +225,11 @@
     )
     block_out = block_float.astype(jnp.bfloat16)
     cls_low = block_out.reshape(span_count, SPAN_LEN, model_width)[:, 0, :]
-    row_cls = lax.all_gather(cls_low, "narrow", axis=0, tiled=True)
-    col_cls = lax.all_gather(cls_low, "wide", axis=0, tiled=True)
-    n_wide = lax.axis_size("wide")
-    n_narrow = lax.axis_size("narrow")
-    wide_at = lax.axis_index("wide")
-    narrow_at = lax.axis_index("narrow")
-    live, has_pair, mate = span_layout(doc_count, single_flag)
-    span_ids = jnp.arange(n_wide * n_narrow * span_count, dtype=jnp.int32)
-    row_ids = row_block(span_ids, wide_at, n_wide, n_narrow)
-    row_pair = row_block(has_pair, wide_at, n_wide, n_narrow)
-    row_mate = row_block(mate, wide_at, n_wide, n_narrow)
-    col_ids = col_block(span_ids, narrow_at, n_wide, n_narrow)
-    col_live = col_block(live, narrow_at, n_wide, n_narrow)
-    sims = score_scale * matmul_right_t(row_cls, col_cls)
-    allowed = col_live[None, :] & (col_ids[None, :] != row_ids[:, None])
-    masked = jnp.where(allowed, sims, far_low)
-    part_top = jnp.max(masked, axis=1)
-    part_total = jnp.sum(jnp.exp(masked - part_top[:, None]), axis=1)
-    row_top, row_total = combined_all((part_top, part_total), "narrow", stats_combine)
-    row_lse = row_top + jnp.log(row_total)
-    matches = col_ids[None, :] == row_mate[:, None]
-    positive = jnp.sum(jnp.where(matches, sims, 0.0), axis=1)
-    row_loss = jnp.where(row_pair, row_lse - positive, 0.0)
-    span_loss = lax.dynamic_slice_in_dim(row_loss, narrow_at * span_count, span_count)
-    loss_part = jnp.sum(span_loss)
-    sim_probs = jnp.exp(masked - row_lse[:, None])
-    sim_grad = jnp.where(row_pair[:, None], sim_probs - matches.astype(jnp.float32), 0.0).astype(
-        jnp.bfloat16
-    )
-    cls_grad = lax.psum_scatter(
-        (score_scale * matmul(sim_grad, col_cls)).astype(jnp.bfloat16),
-        "narrow",
-        scatter_dimension=0,
-        tiled=True,
-    ).astype(jnp.float32)
-    cls_grad = cls_grad + lax.psum_scatter(
-        (score_scale * matmul_left_t(sim_grad, row_cls)).astype(jnp.bfloat16),
-        "wide",
-        scatter_dimension=0,
-        tiled=True,
-    ).astype(jnp.float32)
+    cls_all = lax.all_gather(cls_low, ("wide", "narrow"), axis=0, tiled=True)
+    own = lax.axis_index("wide") * lax.axis_size("narrow") + lax.axis_index("narrow")
+    cls_grad, span_loss, loss_part = contrast(
+        cls_all, doc_count, single_flag, own.astype(jnp.int32), span_count
+    )
     upper_grad = out_grad.astype(jnp.float32).reshape(span_count, SPAN_LEN, model_width)
     top_grad = jnp.concatenate([cls_grad[:, None, :], upper_grad[:, 1:, :]], axis=1).reshape(
         row_count, model_width
@@ -257,40 +278,34 @@
     grad_b_value = jnp.sum(value_grad.astype(jnp.float32), axis=0)
     grad_w_qkv = matmul_left_t(hidden_in, packed_grad)
     grad_in = pre_one_grad + matmul_right_t(packed_grad, w_qkv)
-    (
-        grad_w_qkv,
+    both = ("wide", "narrow")
+    grad_w_ff_out, grad_w_in, grad_w_out, grad_w_qkv = (
+        lax.psum(grad.astype(jnp.bfloat16), both).astype(jnp.float32)
+        for grad in (grad_w_ff_out, grad_w_in, grad_w_out, grad_w_qkv)
+    )
+    vectors = (
         grad_b_query,
         grad_b_value,
-        grad_w_out,
         grad_b_out,
         grad_ln1_gain,
         grad_ln1_bias,
-        grad_w_in,
-        grad_b_in,
-        grad_w_ff_out,
         grad_b_ff_out,
         grad_ln2_gain,
         grad_ln2_bias,
-        loss_part,
-    ) = lax.psum(
-        (
-            grad_w_qkv,
-            grad_b_query,
-            grad_b_value,
-            grad_w_out,
-            grad_b_out,
-            grad_ln1_gain,
-            grad_ln1_bias,
-            grad_w_in,
-            grad_b_in,
-            grad_w_ff_out,
-            grad_b_ff_out,
-            grad_ln2_gain,
-            grad_ln2_bias,
-            loss_part,
-        ),
-        ("wide", "narrow"),
-    )
+        grad_b_in,
+    )
+    joined = lax.psum(jnp.concatenate(vectors), both)
+    (
+        grad_b_query,
+        grad_b_value,
+        grad_b_out,
+        grad_ln1_gain,
+        grad_ln1_bias,
+        grad_b_ff_out,
+        grad_ln2_gain,
+        grad_ln2_bias,
+        grad_b_in,
+    ) = jnp.split(joined, [model_width * k for k in range(1, 9)])
     return (
         block_out,
         loss_part,

time: 835 us -> 529 us (0.63)
  waiting for transfers between devices: 450 us -> 180 us
  local copies, waits for them, and re-layouts: 83.7 us -> 56.9 us
  matrix products: 139 us -> 128 us
    psum x1, waiting for transfers between devices: 374 us -> 180 us  [per_device(): lax.psum(grad.astype(jnp.bfloat16), both).astype(jnp.float32)]
    reduce_scatter x2 -> x0, waiting for transfers between devices: 75.7 us -> none  [the longest x1 61.3 us: per_device(): lax.psum_scatter((score_scale * matmul_left_t(sim_grad, row_cls)).astype(...]
    convert_element_type x0 -> x3, other arithmetic: none -> 17 us  [per_device(): lax.psum(grad.astype(jnp.bfloat16), both).astype(jnp.float32)]
    unnamed x118 -> x132, local copies, waits for them, and re-layouts: 47.8 us -> 34.9 us
    all_gather x2 -> x1, blocking collectives: 39.9 us -> 47 us  [per_device(): cls_all = lax.all_gather(cls_low, ('wide', 'narrow'), axis=0, tiled=True)]
    dot_general x5 -> x4, matrix products: 26.9 us -> 22.7 us  [matmul_left_t(): lax.dot_general(left, right, (((0,), (0,)), ((), ())), preferred_element_...]
    dot_general x5 -> x4, matrix products: 49.7 us -> 46.4 us  [matmul(): return jnp.dot(left, right, preferred_element_type=jnp.float32)]
    dot_general x5 -> x4, matrix products: 44.4 us -> 41.6 us  [matmul_right_t(): lax.dot_general(left, right, (((1,), (1,)), ((), ())), preferred_element_...]
  transfers between devices with their start and end apart: 3 -> 1, of which waited for: 3 -> 1; matrix products, arithmetic and copies ran while one was open for 2% -> 5% of each run, Pallas kernels for 0% -> 0%
where the time goes in v1:
time: 529 us; the launch traced here: 524 us
  waiting for transfers between devices  180 us (34%)
  matrix products  128 us (24%)
  blocking collectives  86.5 us (16%)
  local copies, waits for them, and re-layouts  56.9 us (11%)
  other arithmetic  56.1 us (11%)
  between operations  15.3 us (3%)
    psum x1, waiting for transfers between devices, per_device(): lax.psum(grad.astype(jnp.bfloat16), both).astype(jnp.float32)  180 us
    all_gather x1, blocking collectives, per_device(): cls_all = lax.all_gather(cls_low, ('wide', 'narrow'), axis=0, tiled=True)  47 us
    dot_general x4, matrix products, matmul(): return jnp.dot(left, right, preferred_element_type=jnp.float32)  46.4 us
    dot_general x4, matrix products, matmul_right_t(): lax.dot_general(left, right, (((1,), (1,)), ((), ())), preferred_element_...  41.6 us
    psum x1, blocking collectives, per_device(): joined = lax.psum(jnp.concatenate(vectors), both)  39.6 us
    unnamed x132, local copies, waits for them, and re-layouts  34.9 us
    dot_general x4, matrix products, matmul_left_t(): lax.dot_general(left, right, (((0,), (0,)), ((), ())), preferred_element_...  22.7 us
    convert_element_type x3, other arithmetic, per_device(): lax.psum(grad.astype(jnp.bfloat16), both).astype(jnp.float32)  17 us
  transfers between devices with their start and end apart: 1, of which 1 were waited for; matrix products, arithmetic and copies ran while one was open for 5% of the time, Pallas kernels for 0%

profile of v1, /device:TPU:0, one launch (start us, length us, event | category | flops | bytes accessed | tf_op | source)
XLA Modules:
  0.0 524.1 jit_solution(10973079829767882726)
XLA Ops:
  7.3 1.4 convert_element_type.149
  8.7 1.3 convert_element_type.155
  10.0 1.3 convert_element_type.150
  11.2 1.3 convert_element_type.142
  12.5 1.3 convert_element_type.140
  13.8 1.3 convert_element_type.148
  17.6 1.3 convert_element_type.152
  19.7 3.5 slice_convert_fusion.1
  23.2 3.8 fusion.60
  27.1 1.3 slice.43
  28.4 2.3 fusion.12
  30.7 2.8 copy.49
  33.5 3.0 copy.78
  36.5 2.6 copy.51
  39.0 3.0 copy.80
  42.0 2.6 copy.50
  44.6 2.0 copy.79
  46.6 1.3 multiply_reduce_fusion.1
  48.0 1.7 fusion.6
  50.6 1.4 fusion.28
  53.9 1.7 fusion.58
  56.3 1.9 copy-done.30
  58.2 35.4 %multiply_convert_fusion = (bf16[1024,3072]{1,0:T(8,128)(2,1)S(1)}, f32[1024,3072]{1,0:T(8,128)}, f32[1024,3072]{1,0:T(8,128)}) fusion(f32[3072]{0:T(1024)S(1)} %copy-done.37, bf16[768,3072]{1,0:T(8,128)(2,1)S(1)} %bitcast.127, f32[1024,768]{1,0:T(8,128)S(1)} %get-tuple-element.88, f32[768]{0:T(1024)S(1)} %copy-done.39, f32[768]{0:T(1024)S(1)} %copy-done.30, ...), kind=kOutput, calls=%fused_computation.4 | convolution fusion | flops 5043388416 | bytes 39348224 | tf_op jit(solution)/shard_map/dot_general | solution.py:21
  93.7 5.5 %fusion.59 = (f32[1024]{0:T(1024)S(1)}, f32[1024,768]{1,0:T(8,128)S(1)}) fusion(f32[768]{0:T(1024)S(1)} %copy-done.41, bf16[1024,3072]{1,0:T(8,128)(2,1)S(1)} %get-tuple-element.73, bf16[3072,768]{1,0:T(8,128)(2,1)S(1)} %bitcast.125, f32[768]{0:T(1024)S(1)} %copy-done.39, f32[768]{0:T(1024)S(1)} %copy-done.30, f32[1024]{0:T(1024)S(1)} %add_rsqrt_fusion.1, ...), kind=kOutput, calls=%fused_computation.122 | convolution fusion | flops 4837342208 | bytes 17323008 | tf_op jit(solution)/shard_map/dot_general | solution.py:21
  102.0 47.0 %all-gather = bf16[256,1,768]{2,0,1:T(8,128)(2,1)} all-gather(bf16[8,1,768]{2,0,1:T(8,128)(2,1)S(1)} %copy.77), channel_id=2, replica_groups=mesh['wide'=8,'narrow'=4] {'wide','narrow'}, dimensions={0}, use_global_device_ids=true | all-gather | bytes 405504 | tf_op jit(solution)/shard_map/all_gather | solution.py:228
  150.7 1.3 contrast.1
  152.1 2.6 multiply_reduce_fusion.5
  154.9 1.5 fusion.13
  156.4 2.1 convert_reduce_fusion.1
  158.5 7.0 %convolution_convert_fusion = bf16[3072,768]{1,0:T(8,128)(2,1)} fusion(bf16[1024,3072]{1,0:T(8,128)(2,1)S(1)} %bitcast.130, f32[1024,768]{1,0:T(8,128)S(1)} %get-tuple-element.68), kind=kOutput, calls=%fused_computation.25 | convolution fusion | flops 4834983936 | bytes 14155776 | tf_op jit(solution)/shard_map/dot_general | solution.py:25
  165.6 19.2 %convert_reduce_fusion = (f32[3072]{0:T(1024)}, bf16[1024,3072]{1,0:T(8,128)(2,1)}) fusion(f32[1024,3072]{1,0:T(8,128)} %get-tuple-element.74, bf16[3072,768]{1,0:T(8,128)(2,1)} %param.28, f32[1024,768]{1,0:T(8,128)} %copy-done.16, f32[1024,3072]{1,0:T(8,128)} %get-tuple-element.89, f32[3072]{0:T(1024)S(1)} %copy-done.38), kind=kOutput, calls=%fused_computation.2 | convolution fusion | flops 4886098944 | bytes 39346176 | tf_op jit(solution)/shard_map/dot_general | solution.py:31
  184.9 11.6 %multiply_reduce_fusion.2 = (f32[768]{0:T(1024)}, f32[1024]{0:T(1024)S(1)}, f32[1024]{0:T(1024)S(1)}, f32[768]{0:T(1024)}, f32[1024,768]{1,0:T(8,128)S(1)}) fusion(f32[1024,768]{1,0:T(8,128)} %copy-done.11, f32[1024]{0:T(1024)S(1)} %copy-done.33, f32[1024]{0:T(1024)S(1)} %copy-done.29, f32[768]{0:T(1024)S(1)} %copy-done.31, f32[1024,768]{1,0:T(8,128)} %copy-done.16, ...), kind=kOutput, calls=%fused_computation.41 | convolution fusion | flops 4839698432 | bytes 20472832 | tf_op jit(solution)/shard_map/dot_general | solution.py:31
  196.5 8.0 %convolution_convert_fusion.1 = bf16[768,3072]{1,0:T(8,128)(2,1)} fusion(bf16[1024,3072]{1,0:T(8,128)(2,1)S(1)} %copy-done.48, f32[1024,768]{1,0:T(8,128)S(1)} %copy-done.12, f32[768]{0:T(1024)S(1)} %copy-done.40, f32[768]{0:T(1024)S(1)} %copy-done.31, f32[1024]{0:T(1024)S(1)} %copy-done.33, f32[1024]{0:T(1024)S(1)} %copy-done.29), kind=kOutput, calls=%fused_computation.26 | convolution fusion | flops 4838129664 | bytes 14170112 | tf_op jit(solution)/shard_map/dot_general | solution.py:25
  204.5 1.7 convert_reduce_fusion.2
  206.1 2.4 fusion.25
  208.6 2.6 convolution_convert_fusion.3
  211.2 2.6 copy.60
  213.7 1.9 copy.82
  215.7 5.3 %convert_reduce_fusion.3 = (f32[12,64]{1,0:T(8,128)S(1)}, bf16[8,128,12,64]{1,3,2,0:T(8,128)(2,1)S(1)}) fusion(f32[8,12,128,128]{2,3,1,0:T(8,128)} %copy-done.4, f32[8,12,128]{2,1,0:T(8,128)S(1)} %copy-done.20, bf16[8,128,12,64]{1,0,3,2:T(8,128)(2,1)S(1)} %bitcast.108), kind=kOutput, calls=%fused_computation.43 | convolution fusion | flops 208403712 | bytes 9489408 | tf_op jit(solution)/shard_map/shlm,slhe->smhe/dot_general | solution.py:256
  221.0 6.0 %multiply_reduce_fusion = (f32[8,12,128]{2,1,0:T(8,128)S(1)}, f32[8,12,128,128]{2,3,1,0:T(8,128)}) fusion(f32[8,12,128,128]{2,3,1,0:T(8,128)} %copy-done.4, f32[8,12,128]{2,1,0:T(8,128)S(1)} %copy-done.20, bf16[8,128,12,64]{1,0,3,2:T(8,128)(2,1)S(1)} %bitcast.120, bf16[8,128,12,64]{1,0,3,2:T(8,128)(2,1)S(1)} %bitcast.109), kind=kOutput, calls=%fused_computation.19 | convolution fusion | flops 207605760 | bytes 15826944 | tf_op jit(solution)/shard_map/slhe,smhe->shlm/dot_general | solution.py:259
  227.0 4.9 multiply_convert_fusion.1
  231.9 2.3 fusion.30
  240.2 2.2 copy-done.21
  242.4 5.2 fusion.7
  247.6 1.3 reduce_sum.202
  249.7 1.3 constant_dynamic-update-slice_fusion
  251.0 1.3 constant_dynamic-update-slice_fusion.2
  252.3 1.3 constant_dynamic-update-slice_fusion.1
  253.6 1.3 constant_dynamic-update-slice_fusion.8
  254.9 1.3 constant_dynamic-update-slice_fusion.7
  256.2 1.3 constant_dynamic-update-slice_fusion.6
  257.6 1.3 constant_dynamic-update-slice_fusion.5
  258.9 1.9 fusion.46
  260.8 1.3 constant_dynamic-update-slice_fusion.4
  262.1 1.3 constant_dynamic-update-slice_fusion.3
  263.4 39.6 %psum.36 = f32[9216]{0:T(1024)} all-reduce(f32[9216]{0:T(1024)} %constant_dynamic-update-slice_fusion.3), channel_id=1, replica_groups=mesh['wide'=8,'narrow'=4] {'wide','narrow'}, use_global_device_ids=true, to_apply=%region_22.0 | all-reduce | flops 9216 | bytes 73728 | tf_op jit(solution)/shard_map/psum | solution.py:297
  303.0 1.3 split.41
  304.3 1.4 fusion.57
  305.7 8.2 %convolution_add_fusion.1 = f32[1024,768]{1,0:T(8,128)} fusion(f32[1024,768]{1,0:T(8,128)} %copy-done.15, bf16[1024,2304]{0,1:T(8,128)(2,1)} %copy-done.21, bf16[768,2304]{1,0:T(8,128)(2,1)S(1)} %copy-done), kind=kOutput, calls=%fused_computation.66 | convolution fusion | flops 3624665088 | bytes 14548992 | tf_op jit(solution)/shard_map/dot_general | solution.py:31
  313.9 179.9 %all-reduce.3.cloned.1.call-done = (bf16[768,2304]{0,1:T(8,128)(2,1)}, bf16[768,768]{1,0:T(8,128)(2,1)}, bf16[768,3072]{1,0:T(8,128)(2,1)}, bf16[3072,768]{1,0:T(8,128)(2,1)}) async-done(((bf16[768,2304]{0,1:T(8,128)(2,1)}, bf16[768,768]{1,0:T(8,128)(2,1)}, bf16[768,3072]{1,0:T(8,128)(2,1)}, bf16[3072,768]{1,0:T(8,128)(2,1)}), (bf16[768,2304]{0,1:T(8,128)(2,1)}, bf16[768,768]{1,0:T(8,128)(2,1)}, ...) | async-done | bytes 14155792 | tf_op jit(solution)/shard_map/psum | solution.py:283
  493.8 2.8 convert_element_type.179
  496.6 5.9 %copy.72 = f32[768,2304]{1,0:T(8,128)} copy(bf16[768,2304]{0,1:T(8,128)(2,1)} %get-tuple-element.63) | data formatting | bytes 10616832
  502.6 7.4 %convert_element_type.181 = f32[768,3072]{1,0:T(8,128)} convert(bf16[768,3072]{1,0:T(8,128)(2,1)} %get-tuple-element.65) | non-fusion elementwise | flops 2359296 | bytes 14155776 | tf_op jit(solution)/shard_map/convert_element_type | solution.py:283
  509.9 6.8 %convert_element_type.183 = f32[3072,768]{1,0:T(8,128)} convert(bf16[3072,768]{1,0:T(8,128)(2,1)} %get-tuple-element.66) | non-fusion elementwise | flops 2359296 | bytes 14155776 | tf_op jit(solution)/shard_map/convert_element_type | solution.py:283
  (148 shorter events, 18.3 us)
Async XLA Ops:
  7.2 16.0 %copy-start = (bf16[768,2304]{1,0:T(8,128)(2,1)S(1)}, bf16[768,2304]{1,0:T(8,128)(2,1)}, u32[]{:S(2)}) copy-start(bf16[768,2304]{1,0:T(8,128)(2,1)} %param.19) | copy-start | bytes 10616836
  7.2 486.6 %all-reduce.3.cloned.1.call-start = ((), (), s32[]{:S(2)}) async-start(), calls=%async_computation | async-start | bytes 28311552 | tf_op jit(solution)/shard_map/psum | solution.py:283
  19.7 3.6 copy-start.43
  27.1 1.3 copy-start.35
  27.1 1.3 copy-start.36
  44.6 2.0 copy-start.7
  46.6 1.3 copy-start.9
  47.9 2.7 copy-start.4
  47.9 2.7 copy-start.13
  52.1 1.3 copy-start.42
  52.1 1.4 copy-start.44
  52.1 1.7 copy-start.46
  53.4 2.2 copy-start.18
  53.4 2.9 slice-start.4
  53.9 2.4 slice-start.5
  53.9 39.8 %slice-start.2 = ((s8[4718592]{0:T(1024)(128)(4,1)}), s8[4194304]{0:T(1024)(128)(4,1)S(1)}, s32[]{:S(2)}) async-start(s8[4718592]{0:T(1024)(128)(4,1)} %bitcast.124), calls=%async_computation.3 | async-start | bytes 8388608
  55.6 38.0 %copy-start.11 = (f32[1024,768]{1,0:T(8,128)}, f32[1024,768]{1,0:T(8,128)S(1)}, u32[]{:S(2)}) copy-start(f32[1024,768]{1,0:T(8,128)S(1)} %get-tuple-element.88) | copy-start | bytes 9437188
  55.6 2.6 copy-start.30
  55.6 2.6 copy-start.37
  55.6 2.6 copy-start.39
  55.7 38.0 %copy-start.28 = (f32[1024]{0:T(1024)}, f32[1024]{0:T(1024)S(1)}, u32[]{:S(2)}) copy-start(f32[1024]{0:T(1024)S(1)} %broadcast_multiply_fusion.4) | copy-start | bytes 12292
  58.2 35.4 %copy-start.32 = (f32[1024]{0:T(1024)}, f32[1024]{0:T(1024)S(1)}, u32[]{:S(2)}) copy-start(f32[1024]{0:T(1024)S(1)} %add_rsqrt_fusion.1) | copy-start | bytes 12292
  58.2 35.4 %copy-start.41 = (f32[768]{0:T(1024)S(1)}, f32[768]{0:T(1024)}, u32[]{:S(2)}) copy-start(f32[768]{0:T(1024)} %convert_element_type.154) | copy-start | bytes 9220
  58.2 35.4 %slice-start.3 = ((s8[4718592]{0:T(1024)(128)(4,1)}), s8[524288]{0:T(1024)(128)(4,1)S(1)}, s32[]{:S(2)}) async-start(s8[4718592]{0:T(1024)(128)(4,1)} %bitcast.124), calls=%async_computation.4 | async-start | bytes 1048576
  93.6 5.5 %copy-start.49 = (bf16[1024,3072]{1,0:T(8,128)(2,1)}, bf16[1024,3072]{1,0:T(8,128)(2,1)S(1)}, u32[]{:S(2)}) copy-start(bf16[1024,3072]{1,0:T(8,128)(2,1)S(1)} %get-tuple-element.73) | copy-start | bytes 18874372
  99.1 1.7 copy-start.5
  99.1 0.7 copy-start.22
  99.2 0.8 copy-start.34
  99.2 1.7 copy-start.24
  99.9 2.1 copy-start.26
  100.9 1.1 copy-start.17
  149.0 1.0 copy-start.1
  150.0 0.7 copy-start.3
  152.0 2.6 copy-start.2
  152.0 2.9 copy-start.6
  152.0 2.8 copy-start.23
  152.1 2.8 copy-start.25
  152.1 2.8 copy-start.27
  154.9 3.6 slice-start.6
  156.4 2.1 slice-start.7
  158.5 7.0 %copy-start.16 = (f32[1024,768]{1,0:T(8,128)}, f32[1024,768]{1,0:T(8,128)S(1)}, u32[]{:S(2)}) copy-start(f32[1024,768]{1,0:T(8,128)S(1)} %get-tuple-element.68) | copy-start | bytes 9437188
  158.5 7.0 %copy-start.38 = (f32[3072]{0:T(1024)S(1)}, f32[3072]{0:T(1024)}, u32[]{:S(2)}) copy-start(f32[3072]{0:T(1024)} %convert_element_type.152) | copy-start | bytes 36868
  165.6 19.3 %copy-start.29 = (f32[1024]{0:T(1024)S(1)}, f32[1024]{0:T(1024)}, u32[]{:S(2)}) copy-start(f32[1024]{0:T(1024)} %copy-done.28) | copy-start | bytes 12292
  165.6 19.3 %copy-start.31 = (f32[768]{0:T(1024)S(1)}, f32[768]{0:T(1024)}, u32[]{:S(2)}) copy-start(f32[768]{0:T(1024)} %convert_element_type.149) | copy-start | bytes 9220
  165.6 19.2 %copy-start.33 = (f32[1024]{0:T(1024)S(1)}, f32[1024]{0:T(1024)}, u32[]{:S(2)}) copy-start(f32[1024]{0:T(1024)} %copy-done.32) | copy-start | bytes 12292
  184.8 11.6 %copy-start.12 = (f32[1024,768]{1,0:T(8,128)S(1)}, f32[1024,768]{1,0:T(8,128)}, u32[]{:S(2)}) copy-start(f32[1024,768]{1,0:T(8,128)} %copy-done.11) | copy-start | bytes 9437188
  184.8 11.6 %copy-start.40 = (f32[768]{0:T(1024)S(1)}, f32[768]{0:T(1024)}, u32[]{:S(2)}) copy-start(f32[768]{0:T(1024)} %convert_element_type.150) | copy-start | bytes 9220
  184.8 11.6 %copy-start.48 = (bf16[1024,3072]{1,0:T(8,128)(2,1)S(1)}, bf16[1024,3072]{1,0:T(8,128)(2,1)}, u32[]{:S(2)}) copy-start(bf16[1024,3072]{1,0:T(8,128)(2,1)} %get-tuple-element.100) | copy-start | bytes 18874372
  204.5 1.7 copy-start.19
  206.1 2.4 copy-start.15
  206.1 2.4 copy-start.47
  213.7 1.9 copy-start.20
  215.6 5.3 %copy-start.14 = (bf16[96,8,8,128]{3,2,1,0:T(8,128)(2,1)S(1)}, bf16[96,8,8,128]{3,2,1,0:T(8,128)(2,1)}, u32[]{:S(2)}) copy-start(bf16[96,8,8,128]{3,2,1,0:T(8,128)(2,1)} %copy.78) | copy-start | bytes 4718596
  215.7 11.3 %slice-start = ((s8[6291456]{0:T(1024)(128)(4,1)}), s8[4194304]{0:T(1024)(128)(4,1)S(1)}, s32[]{:S(2)}) async-start(s8[6291456]{0:T(1024)(128)(4,1)} %bitcast.102), calls=%async_computation.1 | async-start | bytes 8388608
  221.0 6.0 %slice-start.1 = ((s8[6291456]{0:T(1024)(128)(4,1)}), s8[2097152]{0:T(1024)(128)(4,1)S(1)}, s32[]{:S(2)}) async-start(s8[6291456]{0:T(1024)(128)(4,1)} %bitcast.102), calls=%async_computation.2 | async-start | bytes 4194304
  227.0 4.9 copy-start.10
  231.9 2.3 copy-start.8
  239.4 3.0 copy-start.45
  240.2 2.2 copy-start.21
Sparse Core Ops, SparseCore 0:
  247.8 245.9 all-reduce.2

commit v2 on v1

--- a/solution.py
+++ b/solution.py
@@ -165,6 +165,184 @@
     return cls_grad, own_loss.reshape(-1), loss.reshape(())
 
 
+MESH = pl.DeviceIdType.MESH
+TICKS = 6
+
+def ar_kernel(n_x, n_z, ffo_ref, in_ref, out_ref, qkv_ref, vec_ref, o_ffo, o_rest, o_vec, part, sib, r1, r2, r3, vbuf, lsem, s_sem, r_sem, zs_sem, zr_sem, vs_sem, vr_sem):
+    W = part.shape[2]
+    H, Q = W // 2, W // 4
+    E = Q // n_z
+    wide, narrow = lax.axis_index("wide"), lax.axis_index("narrow")
+    z, x = wide // n_x, wide % n_x
+    y, c = narrow // 2, narrow % 2
+    f32 = jnp.float32
+    core = (wide, y * 2 + 1 - c)
+    near_x = (z * n_x + 1 - x, narrow)
+    near_y = (wide, (1 - y) * 2 + c)
+    one = (jnp.where(c == 0, near_x[0], near_y[0]), jnp.where(c == 0, near_x[1], near_y[1]))
+    two = (jnp.where(c == 0, near_y[0], near_x[0]), jnp.where(c == 0, near_y[1], near_x[1]))
+    h1 = jnp.where(c == 0, x, y)
+    h2 = jnp.where(c == 0, y, x)
+    others = [lax.rem(z + k, n_z) for k in range(1, n_z)]
+    zdev = [(o * n_x + x, narrow) for o in others]
+
+    bar = pltpu.get_barrier_semaphore()
+    for d in [core, near_x, near_y] + zdev:
+        pl.semaphore_signal(bar, inc=1, device_id=d, device_id_type=MESH)
+
+    loads = []
+    for b in range(2 * TICKS):
+        if b < 4:
+            src = ffo_ref.at[pl.ds(b * W, W), :]
+        elif b < 8:
+            src = in_ref.at[:, pl.ds((b - 4) * W, W)]
+        elif b < 9:
+            src = out_ref
+        else:
+            src = qkv_ref.at[:, pl.ds((b - 9) * W, W)]
+        cp = pltpu.make_async_copy(src, part.at[b], lsem.at[b])
+        cp.start()
+        loads.append(cp)
+    pl.semaphore_wait(bar, 2 + n_z)
+
+    def out_at(t, row, rows):
+        if t < 2:
+            return o_ffo.at[pl.ds(pl.multiple_of((2 * t + c) * W + row, 16), rows), :]
+        return o_rest.at[pl.ds(pl.multiple_of(row, 16), rows), pl.ds(pl.multiple_of((2 * (t - 2) + c) * W, 128), W)]
+
+    def rcopy(src, dst, k, t, dev):
+        return pltpu.make_async_remote_copy(src, dst, s_sem.at[k, t], r_sem.at[k, t], device_id=dev, device_id_type=MESH)
+
+    def add(t, row, rows, got):
+        mine = 2 * t + c
+        def body(i, _):
+            at = pl.multiple_of(row + i * 48, 16)
+            here = part[mine, pl.ds(at, 48), :].astype(f32) + got[pl.ds(pl.multiple_of(i * 48, 16), 48), :].astype(f32)
+            part[mine, pl.ds(at, 48), :] = here.astype(jnp.bfloat16)
+            return 0
+        lax.fori_loop(0, rows // 48, body, 0)
+
+    keep1 = h1 * H
+    keep2 = keep1 + h2 * Q
+    own = keep2 + z * E
+    flight = {}
+    def c0(t):
+        return rcopy(part.at[2 * t + 1 - c], sib.at[t], 0, t, core)
+    def c1(t):
+        return rcopy(part.at[2 * t + c, pl.ds(pl.multiple_of((1 - h1) * H, 16), H), :], r1.at[t], 1, t, one)
+    def c2(t):
+        return rcopy(part.at[2 * t + c, pl.ds(pl.multiple_of(keep1 + (1 - h2) * Q, 16), Q), :], r2.at[t], 2, t, two)
+    def c3(t):
+        return [pltpu.make_async_remote_copy(
+            part.at[2 * t + c, pl.ds(pl.multiple_of(keep2 + o * E, 16), E), :], r3.at[t, k],
+            zs_sem.at[0, t, k], zr_sem.at[0, t, k], device_id=d, device_id_type=MESH)
+            for k, (o, d) in enumerate(zip(others, zdev))]
+    def c4(t):
+        return [pltpu.make_async_remote_copy(
+            out_at(t, own, E), out_at(t, own, E), zs_sem.at[1, t, k], zr_sem.at[1, t, k], device_id=d, device_id_type=MESH)
+            for k, d in enumerate(zdev)]
+    def c5(t):
+        return rcopy(out_at(t, keep2, Q), out_at(t, keep2, Q), 3, t, two)
+    def c6(t):
+        return rcopy(out_at(t, keep1, H), out_at(t, keep1, H), 4, t, one)
+    def c7(t):
+        return rcopy(out_at(t, 0, W), out_at(t, 0, W), 5, t, core)
+
+    def st0(t):
+        loads[2 * t].wait(); loads[2 * t + 1].wait()
+        c0(t).start()
+    def st1(t):
+        c0(t).wait()
+        add(t, 0, W, sib.at[t])
+        c1(t).start()
+    def st2(t):
+        c1(t).wait()
+        add(t, keep1, H, r1.at[t])
+        c2(t).start()
+    def st3(t):
+        c2(t).wait()
+        add(t, keep2, Q, r2.at[t])
+        for cp in c3(t): cp.start()
+    def st4(t):
+        for cp in c3(t): cp.wait()
+        total = part[2 * t + c, pl.ds(pl.multiple_of(own, 16), E), :].astype(f32)
+        for k in range(n_z - 1):
+            total = total + r3[t, k].astype(f32)
+        part[2 * t + c, pl.ds(pl.multiple_of(own, 16), E), :] = total.astype(jnp.bfloat16)
+        cp = pltpu.make_async_copy(part.at[2 * t + c, pl.ds(pl.multiple_of(own, 16), E), :], out_at(t, own, E), lsem.at[2 * TICKS + t])
+        cp.start(); cp.wait()
+        for cp in c4(t): cp.start()
+    def st5(t):
+        for cp in c4(t): cp.wait()
+        c5(t).start()
+    def st6(t):
+        c5(t).wait()
+        c6(t).start()
+    def st7(t):
+        c6(t).wait()
+        c7(t).start()
+    def st8(t):
+        c7(t).wait()
+
+    def vcopy(k, dev):
+        return pltpu.make_async_remote_copy(vbuf.at[2 * k], vbuf.at[2 * k + 1], vs_sem.at[k], vr_sem.at[k], device_id=dev, device_id_type=MESH)
+    def vz():
+        return [pltpu.make_async_remote_copy(vbuf.at[6], vbuf.at[7 + k], vs_sem.at[3 + k], vr_sem.at[3 + k], device_id=d, device_id_type=MESH) for k, d in enumerate(zdev)]
+    def vstep(k):
+        if k == 0:
+            vbuf[0] = vec_ref[...]
+            vcopy(0, core).start()
+        elif k == 1:
+            vcopy(0, core).wait()
+            vbuf[2] = vbuf[0] + vbuf[1]
+            vcopy(1, near_x).start()
+        elif k == 2:
+            vcopy(1, near_x).wait()
+            vbuf[4] = vbuf[2] + vbuf[3]
+            vcopy(2, near_y).start()
+        elif k == 3:
+            vcopy(2, near_y).wait()
+            vbuf[6] = vbuf[4] + vbuf[5]
+            for cp in vz(): cp.start()
+        elif k == 4:
+            for cp in vz(): cp.wait()
+            total = vbuf[6]
+            for k in range(n_z - 1):
+                total = total + vbuf[7 + k]
+            o_vec[...] = total
+
+    stages = [st1, st2, st3, st4, st5, st6, st7, st8]
+    for t in range(TICKS):
+        st0(t)
+    for step in range(TICKS + len(stages) - 1):
+        if step >= 2: vstep(step - 2)
+        for k, st in enumerate(stages):
+            if 0 <= step - k < TICKS:
+                st(step - k)
+
+def all_reduce(ffo, inn, out, qkv, vec, n_x, n_z):
+    W = ffo.shape[1]
+    rest = jax.ShapeDtypeStruct((W, 8 * W), jnp.bfloat16)
+    bf = jnp.bfloat16
+    anyspec = pl.BlockSpec(memory_space=pl.ANY)
+    vm = pl.BlockSpec(memory_space=pltpu.VMEM)
+    T = TICKS
+    return pl.pallas_call(
+        functools.partial(ar_kernel, n_x, n_z),
+        out_shape=(jax.ShapeDtypeStruct(ffo.shape, bf), jax.ShapeDtypeStruct(rest.shape, bf), jax.ShapeDtypeStruct(vec.shape, jnp.float32)),
+        in_specs=[anyspec, anyspec, anyspec, anyspec, vm], out_specs=(anyspec, anyspec, vm),
+        scratch_shapes=[
+            pltpu.VMEM((2 * T, W, W), bf), pltpu.VMEM((T, W, W), bf), pltpu.VMEM((T, W // 2, W), bf), pltpu.VMEM((T, W // 4, W), bf),
+            pltpu.VMEM((T, n_z - 1, W // 4 // n_z, W), bf), pltpu.VMEM((6 + n_z,) + vec.shape, jnp.float32),
+            pltpu.SemaphoreType.DMA((3 * T,)), pltpu.SemaphoreType.DMA((6, T)), pltpu.SemaphoreType.DMA((6, T)),
+            pltpu.SemaphoreType.DMA((2, T, n_z - 1)), pltpu.SemaphoreType.DMA((2, T, n_z - 1)),
+            pltpu.SemaphoreType.DMA((2 + n_z,)), pltpu.SemaphoreType.DMA((2 + n_z,)),
+        ],
+        compiler_params=pltpu.CompilerParams(collective_id=0, has_side_effects=True, vmem_limit_bytes=56 * 2**20),
+        name="grad_all_reduce",
+    )(ffo, inn, out, qkv, vec)
+
+
 def per_device(
     hidden_in,
     out_grad,
@@ -279,10 +457,9 @@
     grad_w_qkv = matmul_left_t(hidden_in, packed_grad)
     grad_in = pre_one_grad + matmul_right_t(packed_grad, w_qkv)
     both = ("wide", "narrow")
-    grad_w_ff_out, grad_w_in, grad_w_out, grad_w_qkv = (
-        lax.psum(grad.astype(jnp.bfloat16), both).astype(jnp.float32)
-        for grad in (grad_w_ff_out, grad_w_in, grad_w_out, grad_w_qkv)
-    )
+    weights = [
+        grad.astype(jnp.bfloat16) for grad in (grad_w_ff_out, grad_w_in, grad_w_out, grad_w_qkv)
+    ]
     vectors = (
         grad_b_query,
         grad_b_value,
@@ -294,7 +471,24 @@
         grad_ln2_bias,
         grad_b_in,
     )
-    joined = lax.psum(jnp.concatenate(vectors), both)
+    joined = jnp.concatenate(vectors)
+    n_wide, n_narrow = lax.axis_size("wide"), lax.axis_size("narrow")
+    n_x = n_narrow // 2
+    n_z = n_wide // n_x
+    if n_x == 2 and n_wide % n_x == 0 and model_width % (64 * n_z) == 0 and w_in.shape[1] == 4 * model_width:
+        filled = jnp.pad(joined, (0, 4 * model_width)).reshape(16, model_width)
+        grad_w_ff_out, rest, filled = all_reduce(*weights, filled, n_x, n_z)
+        joined = filled.reshape(-1)[: joined.shape[0]]
+        wide_in = w_in.shape[1]
+        grad_w_in = rest[:, :wide_in].astype(jnp.float32)
+        grad_w_out = rest[:, wide_in : wide_in + model_width].astype(jnp.float32)
+        grad_w_qkv = rest[:, wide_in + model_width :].astype(jnp.float32)
+        grad_w_ff_out = grad_w_ff_out.astype(jnp.float32)
+    else:
+        grad_w_ff_out, grad_w_in, grad_w_out, grad_w_qkv = (
+            lax.psum(grad, both).astype(jnp.float32) for grad in weights
+        )
+        joined = lax.psum(joined, both)
     (
         grad_b_query,
         grad_b_value,

time: 529 us -> 435 us (0.82)
  waiting for transfers between devices: 180 us -> 0 us
  Pallas kernels: 1.34 us -> 134 us
  blocking collectives: 86.5 us -> 44.3 us
  between operations: 15.3 us -> 1.81 us
    psum x1 -> x0, waiting for transfers between devices: 180 us -> none  [per_device(): lax.psum(grad.astype(jnp.bfloat16), both).astype(jnp.float32)]
    pallas_call x0 -> x1, Pallas kernels: none -> 133 us  [all_reduce(): pl.pallas_call(functools.partial(ar_kernel, n_x, n_z), out_shape=(jax.Sha...]
    psum x1 -> x0, blocking collectives: 39.6 us -> none  [per_device(): joined = lax.psum(jnp.concatenate(vectors), both)]
    unnamed x132 -> x141, local copies, waits for them, and re-layouts: 34.9 us -> 26 us
    convert_element_type x3 -> x4, other arithmetic: 17 us -> 18.9 us  [the longest x1 7.4 us: per_device(): grad_w_ff_out = grad_w_ff_out.astype(jnp.float32)]
  transfers between devices with their start and end apart: 1 -> 0, of which waited for: 1 -> 0; matrix products, arithmetic and copies ran while one was open for 5% -> 0% of each run, Pallas kernels for 0% -> 0%
where the time goes in v2:
time: 435 us; the launch traced here: 428 us
  Pallas kernels  134 us (31%)
  matrix products  130 us (30%)
  other arithmetic  59.4 us (14%)
  local copies, waits for them, and re-layouts  58.4 us (13%)
  blocking collectives  44.3 us (10%)
    pallas_call x1, Pallas kernels, all_reduce(): pl.pallas_call(functools.partial(ar_kernel, n_x, n_z), out_shape=(jax.Sha...  133 us
    dot_general x4, matrix products, matmul(): return jnp.dot(left, right, preferred_element_type=jnp.float32)  46.2 us
    all_gather x1, blocking collectives, per_device(): cls_all = lax.all_gather(cls_low, ('wide', 'narrow'), axis=0, tiled=True)  44.3 us
    dot_general x4, matrix products, matmul_right_t(): lax.dot_general(left, right, (((1,), (1,)), ((), ())), preferred_element_...  36.5 us
    unnamed x141, local copies, waits for them, and re-layouts  26 us
    dot_general x4, matrix products, matmul_left_t(): lax.dot_general(left, right, (((0,), (0,)), ((), ())), preferred_element_...  25.9 us

profile of v2, /device:TPU:0, one launch (start us, length us, event | category | flops | bytes accessed | tf_op | source)
XLA Modules:
  0.0 427.8 jit_solution(15107860466710142210)
XLA Ops:
  0.7 1.4 convert_element_type.150
  3.4 1.3 convert_element_type.151
  4.7 2.5 fusion.46
  7.2 1.3 convert_element_type.143
  8.4 1.3 convert_element_type.141
  13.5 1.3 convert_element_type.153
  15.6 3.5 slice_convert_fusion.3
  19.1 3.8 fusion.59
  23.0 1.3 slice.78
  24.3 2.3 fusion.12
  26.6 2.8 copy.49
  29.4 3.0 copy.79
  32.4 2.6 copy.51
  35.0 3.1 copy.81
  38.0 2.6 copy.50
  40.6 2.0 copy.80
  42.6 1.3 multiply_reduce_fusion.1
  43.9 1.7 fusion.6
  46.6 1.4 fusion.28
  49.9 1.7 fusion.57
  52.3 1.9 copy-done.37
  54.2 35.2 %multiply_convert_fusion = (bf16[1024,3072]{1,0:T(8,128)(2,1)S(1)}, f32[1024,3072]{1,0:T(8,128)}, f32[1024,3072]{1,0:T(8,128)}) fusion(f32[3072]{0:T(1024)S(1)} %copy-done.44, bf16[768,3072]{1,0:T(8,128)(2,1)S(1)} %bitcast.127, f32[1024,768]{1,0:T(8,128)S(1)} %get-tuple-element.56, f32[768]{0:T(1024)S(1)} %copy-done.46, f32[768]{0:T(1024)S(1)} %copy-done.37, ...), kind=kOutput, calls=%fused_computation.4 | convolution fusion | flops 5043388416 | bytes 39348224 | tf_op jit(solution)/shard_map/dot_general | solution.py:21
  89.5 5.5 %fusion.58 = (f32[1024]{0:T(1024)S(1)}, f32[1024,768]{1,0:T(8,128)S(1)}) fusion(f32[768]{0:T(1024)S(1)} %copy-done.48, bf16[1024,3072]{1,0:T(8,128)(2,1)S(1)} %get-tuple-element.49, bf16[3072,768]{1,0:T(8,128)(2,1)S(1)} %bitcast.125, f32[768]{0:T(1024)S(1)} %copy-done.46, f32[768]{0:T(1024)S(1)} %copy-done.37, f32[1024]{0:T(1024)S(1)} %add_rsqrt_fusion.1, ...), kind=kOutput, calls=%fused_computation.132 | convolution fusion | flops 4837342208 | bytes 17323008 | tf_op jit(solution)/shard_map/dot_general | solution.py:21
  96.8 44.3 %all-gather = bf16[256,1,768]{2,0,1:T(8,128)(2,1)S(1)} all-gather(bf16[8,1,768]{2,0,1:T(8,128)(2,1)S(1)} %copy.78), channel_id=2, replica_groups=mesh['wide'=8,'narrow'=4] {'wide','narrow'}, dimensions={0}, use_global_device_ids=true | all-gather | bytes 405504 | tf_op jit(solution)/shard_map/all_gather | solution.py:406
  141.1 1.3 contrast.1
  143.0 1.3 reduce_sum.202
  145.2 2.6 multiply_reduce_fusion.5
  148.0 1.5 fusion.13
  149.5 3.0 convert_reduce_fusion.1
  152.5 19.4 %convert_reduce_fusion = (f32[3072]{0:T(1024)}, bf16[1024,3072]{1,0:T(8,128)(2,1)}) fusion(f32[1024,3072]{1,0:T(8,128)} %get-tuple-element.50, bf16[3072,768]{1,0:T(8,128)(2,1)} %param.28, f32[1024,768]{1,0:T(8,128)} %get-tuple-element.44, f32[1024,3072]{1,0:T(8,128)} %get-tuple-element.57, f32[3072]{0:T(1024)S(1)} %copy-done.45), kind=kOutput, calls=%fused_computation.2 | convolution fusion | flops 4886098944 | bytes 39346176 | tf_op jit(solution)/shard_map/dot_general | solution.py:31
  171.9 10.0 %convolution_convert_fusion.1.ffo_ref = bf16[3072,768]{1,0:T(8,128)(2,1)} fusion(bf16[1024,3072]{1,0:T(8,128)(2,1)} %copy-done.56, f32[1024,768]{1,0:T(8,128)} %get-tuple-element.44), kind=kOutput, calls=%fused_computation.26 | convolution fusion | flops 4834983936 | bytes 14155776 | tf_op jit(solution)/shard_map/dot_general | solution.py:25
  182.0 9.0 %multiply_reduce_fusion.2 = (f32[768]{0:T(1024)}, f32[1024]{0:T(1024)S(1)}, f32[1024]{0:T(1024)S(1)}, f32[768]{0:T(1024)}, f32[1024,768]{1,0:T(8,128)S(1)}) fusion(f32[1024,768]{1,0:T(8,128)S(1)} %copy-done.13, f32[1024]{0:T(1024)S(1)} %copy-done.40, f32[1024]{0:T(1024)S(1)} %copy-done.34, f32[768]{0:T(1024)S(1)} %copy-done.38, ...), kind=kOutput, calls=%fused_computation.43 | convolution fusion | flops 4839698432 | bytes 20472832 | tf_op jit(solution)/shard_map/dot_general | solution.py:31
  191.0 7.9 %convolution_convert_fusion.in_ref = bf16[768,3072]{1,0:T(8,128)(2,1)} fusion(bf16[1024,3072]{1,0:T(8,128)(2,1)S(1)} %copy-done.55, f32[1024,768]{1,0:T(8,128)S(1)} %copy-done.13, f32[768]{0:T(1024)S(1)} %copy-done.47, f32[768]{0:T(1024)S(1)} %copy-done.38, f32[1024]{0:T(1024)S(1)} %copy-done.40, f32[1024]{0:T(1024)S(1)} %copy-done.34), kind=kOutput, calls=%fused_computation.25 | convolution fusion | flops 4838129664 | bytes 14170112 | tf_op jit(solution)/shard_map/dot_general | solution.py:25
  198.9 1.7 convert_reduce_fusion.2
  200.6 2.4 fusion.25.out_ref
  203.0 2.6 convolution_convert_fusion.3
  205.6 2.6 copy.60
  208.2 1.9 copy.83
  210.1 6.8 %convert_reduce_fusion.3 = (f32[12,64]{1,0:T(8,128)S(1)}, bf16[8,128,12,64]{1,3,2,0:T(8,128)(2,1)}) fusion(f32[8,12,128,128]{2,3,1,0:T(8,128)} %copy-done.3, f32[8,12,128]{2,1,0:T(8,128)S(1)} %copy-done.25, bf16[8,128,12,64]{1,0,3,2:T(8,128)(2,1)S(1)} %bitcast.108), kind=kOutput, calls=%fused_computation.45 | convolution fusion | flops 208403712 | bytes 9489408 | tf_op jit(solution)/shard_map/shlm,slhe->smhe/dot_general | solution.py:434
  217.5 3.9 copy.71
  221.5 6.3 %multiply_reduce_fusion = (f32[8,12,128]{2,1,0:T(8,128)S(1)}, f32[8,12,128,128]{2,3,1,0:T(8,128)}) fusion(f32[8,12,128,128]{2,3,1,0:T(8,128)} %copy-done.3, f32[8,12,128]{2,1,0:T(8,128)} %log_add_fusion, bf16[8,128,12,64]{1,0,3,2:T(8,128)(2,1)S(1)} %bitcast.120, bf16[8,128,12,64]{1,0,3,2:T(8,128)(2,1)S(1)} %bitcast.109), kind=kOutput, calls=%fused_computation.19 | convolution fusion | flops 207605760 | bytes 15826944 | tf_op jit(solution)/shard_map/slhe,smhe->shlm/dot_general | solution.py:437
  227.8 4.9 %multiply_convert_fusion.1 = bf16[8,12,128,128]{2,3,1,0:T(8,128)(2,1)S(1)} fusion(f32[8,12,128,128]{2,3,1,0:T(8,128)} %get-tuple-element.62, f32[8,12,128,128]{2,3,1,0:T(8,128)S(1)} %bitcast.103, f32[8,12,128]{2,1,0:T(8,128)S(1)} %get-tuple-element.61, f32[8,12,128]{2,1,0:T(8,128)S(1)} %copy-done.26), kind=kLoop, calls=%fused_computation.18 | loop fusion | flops 7864320 | bytes 15826944 | tf_op jit(solution)/shard_map/convert_element_type | solution.py:442
  232.8 3.4 fusion.30
  236.2 2.2 convert_reduce_fusion.4
  239.0 1.3 constant_dynamic-update-slice_fusion
  240.3 1.3 constant_dynamic-update-slice_fusion.2
  241.6 1.3 constant_dynamic-update-slice_fusion.1
  242.9 1.3 constant_dynamic-update-slice_fusion.8
  244.2 1.3 constant_dynamic-update-slice_fusion.7
  245.5 1.3 constant_dynamic-update-slice_fusion.6
  246.8 1.3 constant_dynamic-update-slice_fusion.5
  248.1 1.3 constant_dynamic-update-slice_fusion.4
  249.4 1.3 constant_dynamic-update-slice_fusion.3
  250.7 3.8 copy.68
  255.1 1.4 reshape.179.vec_ref
  256.5 2.8 copy.65
  261.8 5.6 %convolution_add_fusion.1 = f32[1024,768]{1,0:T(8,128)} fusion(f32[1024,768]{1,0:T(8,128)S(1)} %copy-done.20, bf16[1024,2304]{0,1:T(8,128)(2,1)S(1)} %bitcast_dynamic-update-slice_fusion, bf16[768,2304]{1,0:T(8,128)(2,1)S(1)} %copy-done), kind=kOutput, calls=%fused_computation.68 | convolution fusion | flops 3624665088 | bytes 14548992 | tf_op jit(solution)/shard_map/dot_general | solution.py:31
  267.3 5.6 %fusion.7.qkv_ref = bf16[768,2304]{1,0:T(8,128)(2,1)} fusion(bf16[1024,2304]{0,1:T(8,128)(2,1)S(1)} %bitcast_dynamic-update-slice_fusion, bf16[1024,768]{1,0:T(8,128)(2,1)S(1)} %copy-done.52), kind=kOutput, calls=%fused_computation.29 | convolution fusion | flops 3625648128 | bytes 9830400 | tf_op jit(solution)/shard_map/dot_general | solution.py:25
  272.9 132.5 %grad_all_reduce.1 = (bf16[3072,768]{1,0:T(8,128)(2,1)}, bf16[768,6144]{1,0:T(8,128)(2,1)}, f32[16,768]{1,0:T(8,128)}) custom-call(bf16[3072,768]{1,0:T(8,128)(2,1)} %convolution_convert_fusion.1.ffo_ref, bf16[768,3072]{1,0:T(8,128)(2,1)} %convolution_convert_fusion.in_ref, bf16[768,768]{1,0:T(8,128)(2,1)} %fusion.25.out_ref, ...), custom_call_target="tpu_custom_call" | custom-call | tf_op jit(solution)/shard_map/grad_all_reduce/pallas_call | solution.py:330
  406.2 1.7 slice_reduce_fusion
  408.5 2.8 slice_convert_fusion.4
  411.4 7.4 %convert_element_type.184 = f32[3072,768]{1,0:T(8,128)} convert(bf16[3072,768]{1,0:T(8,128)(2,1)} %get-tuple-element.28) | non-fusion elementwise | flops 2359296 | bytes 14155776 | tf_op jit(solution)/shard_map/convert_element_type | solution.py:486
  418.8 3.6 slice_convert_fusion.1
  422.4 5.0 %slice_convert_fusion = f32[768,3072]{1,0:T(8,128)} fusion(bf16[768,6144]{1,0:T(8,128)(2,1)S(1)} %copy-done.14), kind=kLoop, calls=%fused_computation.28 | loop fusion | flops 2359296 | bytes 14155776 | tf_op jit(solution)/shard_map/convert_element_type | solution.py:483
  (157 shorter events, 18.5 us)
Async XLA Ops:
  0.7 18.5 %copy-start = (bf16[768,2304]{1,0:T(8,128)(2,1)S(1)}, bf16[768,2304]{1,0:T(8,128)(2,1)}, u32[]{:S(2)}) copy-start(bf16[768,2304]{1,0:T(8,128)(2,1)} %param.19) | copy-start | bytes 10616836
  15.6 3.6 copy-start.50
  23.0 1.3 copy-start.42
  23.0 1.3 copy-start.43
  40.6 2.0 copy-start.6
  42.6 1.3 copy-start.8
  43.9 2.7 copy-start.3
  43.9 2.7 copy-start.17
  48.1 1.3 copy-start.49
  48.1 1.4 copy-start.51
  48.1 1.7 copy-start.53
  49.4 2.2 copy-start.23
  49.4 2.9 slice-start.4
  49.9 2.4 slice-start.5
  49.9 39.6 %slice-start.2 = ((s8[4718592]{0:T(1024)(128)(4,1)}), s8[4194304]{0:T(1024)(128)(4,1)S(1)}, s32[]{:S(2)}) async-start(s8[4718592]{0:T(1024)(128)(4,1)} %bitcast.124), calls=%async_computation.2 | async-start | bytes 8388608
  51.6 37.9 %copy-start.12 = (f32[1024,768]{1,0:T(8,128)}, f32[1024,768]{1,0:T(8,128)S(1)}, u32[]{:S(2)}) copy-start(f32[1024,768]{1,0:T(8,128)S(1)} %get-tuple-element.56) | copy-start | bytes 9437188
  51.6 2.6 copy-start.37
  51.6 2.6 copy-start.44
  51.6 2.6 copy-start.46
  51.6 37.8 %copy-start.33 = (f32[1024]{0:T(1024)}, f32[1024]{0:T(1024)S(1)}, u32[]{:S(2)}) copy-start(f32[1024]{0:T(1024)S(1)} %broadcast_multiply_fusion.4) | copy-start | bytes 12292
  54.2 35.2 %copy-start.39 = (f32[1024]{0:T(1024)}, f32[1024]{0:T(1024)S(1)}, u32[]{:S(2)}) copy-start(f32[1024]{0:T(1024)S(1)} %add_rsqrt_fusion.1) | copy-start | bytes 12292
  54.2 35.3 %copy-start.48 = (f32[768]{0:T(1024)S(1)}, f32[768]{0:T(1024)}, u32[]{:S(2)}) copy-start(f32[768]{0:T(1024)} %convert_element_type.155) | copy-start | bytes 9220
  54.2 35.3 %slice-start.3 = ((s8[4718592]{0:T(1024)(128)(4,1)}), s8[524288]{0:T(1024)(128)(4,1)S(1)}, s32[]{:S(2)}) async-start(s8[4718592]{0:T(1024)(128)(4,1)} %bitcast.124), calls=%async_computation.3 | async-start | bytes 1048576
  89.4 5.5 %copy-start.56 = (bf16[1024,3072]{1,0:T(8,128)(2,1)}, bf16[1024,3072]{1,0:T(8,128)(2,1)S(1)}, u32[]{:S(2)}) copy-start(bf16[1024,3072]{1,0:T(8,128)(2,1)S(1)} %get-tuple-element.49) | copy-start | bytes 18874372
  95.0 1.8 copy-start.4
  95.0 0.7 copy-start.27
  95.0 0.8 copy-start.41
  95.0 1.7 copy-start.29
  95.5 45.6 %copy-start.2 = (s32[32]{0:T(128)S(1)}, s32[32]{0:T(128)}, u32[]{:S(2)}) copy-start(s32[32]{0:T(128)} %param.32) | copy-start | bytes 388
  95.8 45.3 %copy-start.31 = (f32[1024]{0:T(1024)}, f32[1024]{0:T(1024)S(1)}, u32[]{:S(2)}) copy-start(f32[1024]{0:T(1024)S(1)} %add_rsqrt_fusion) | copy-start | bytes 12292
  96.7 44.4 %copy-start.22 = (bf16[1024,768]{1,0:T(8,128)(2,1)}, bf16[1024,768]{1,0:T(8,128)(2,1)S(1)}, u32[]{:S(2)}) copy-start(bf16[1024,768]{1,0:T(8,128)(2,1)S(1)} %add_convert_fusion.1) | copy-start | bytes 4718596
  142.4 0.6 copy-start.1
  145.1 2.9 copy-start.5
  145.1 2.8 copy-start.28
  145.2 2.8 copy-start.30
  145.2 2.8 copy-start.32
  149.5 3.0 copy-start.45
  171.9 10.1 %copy-start.13 = (f32[1024,768]{1,0:T(8,128)S(1)}, f32[1024,768]{1,0:T(8,128)}, u32[]{:S(2)}) copy-start(f32[1024,768]{1,0:T(8,128)} %copy-done.12) | copy-start | bytes 9437188
  171.9 10.1 %copy-start.21 = (f32[1024,768]{1,0:T(8,128)S(1)}, f32[1024,768]{1,0:T(8,128)}, u32[]{:S(2)}) copy-start(f32[1024,768]{1,0:T(8,128)} %get-tuple-element.44) | copy-start | bytes 9437188
  171.9 10.1 %copy-start.34 = (f32[1024]{0:T(1024)S(1)}, f32[1024]{0:T(1024)}, u32[]{:S(2)}) copy-start(f32[1024]{0:T(1024)} %copy-done.33) | copy-start | bytes 12292
  171.9 10.1 %copy-start.38 = (f32[768]{0:T(1024)S(1)}, f32[768]{0:T(1024)}, u32[]{:S(2)}) copy-start(f32[768]{0:T(1024)} %convert_element_type.150) | copy-start | bytes 9220
  171.9 10.1 %copy-start.40 = (f32[1024]{0:T(1024)S(1)}, f32[1024]{0:T(1024)}, u32[]{:S(2)}) copy-start(f32[1024]{0:T(1024)} %copy-done.39) | copy-start | bytes 12292
  171.9 10.1 %copy-start.55 = (bf16[1024,3072]{1,0:T(8,128)(2,1)S(1)}, bf16[1024,3072]{1,0:T(8,128)(2,1)}, u32[]{:S(2)}) copy-start(bf16[1024,3072]{1,0:T(8,128)(2,1)} %get-tuple-element.68) | copy-start | bytes 18874372
  182.0 9.0 %copy-start.47 = (f32[768]{0:T(1024)S(1)}, f32[768]{0:T(1024)}, u32[]{:S(2)}) copy-start(f32[768]{0:T(1024)} %convert_element_type.151) | copy-start | bytes 9220
  198.9 1.7 copy-start.24
  200.6 2.4 copy-start.19
  200.6 2.4 copy-start.54
  208.2 1.9 copy-start.25
  210.1 6.8 %copy-start.10 = (bf16[96,8,8,128]{3,2,1,0:T(8,128)(2,1)}, bf16[96,8,8,128]{3,2,1,0:T(8,128)(2,1)S(1)}, u32[]{:S(2)}) copy-start(bf16[96,8,8,128]{3,2,1,0:T(8,128)(2,1)S(1)} %copy.83) | copy-start | bytes 4718596
  217.5 4.0 copy-start.11
  217.5 4.0 copy-start.18
  221.5 6.3 %slice-start = ((s8[6291456]{0:T(1024)(128)(4,1)}), s8[4194304]{0:T(1024)(128)(4,1)S(1)}, s32[]{:S(2)}) async-start(s8[6291456]{0:T(1024)(128)(4,1)} %bitcast.102), calls=%async_computation | async-start | bytes 8388608
  221.5 6.3 %slice-start.1 = ((s8[6291456]{0:T(1024)(128)(4,1)}), s8[2097152]{0:T(1024)(128)(4,1)S(1)}, s32[]{:S(2)}) async-start(s8[6291456]{0:T(1024)(128)(4,1)} %bitcast.102), calls=%async_computation.1 | async-start | bytes 4194304
  221.5 6.3 %copy-start.26 = (f32[8,12,128]{2,1,0:T(8,128)S(1)}, f32[8,12,128]{2,1,0:T(8,128)}, u32[]{:S(2)}) copy-start(f32[8,12,128]{2,1,0:T(8,128)} %log_add_fusion) | copy-start | bytes 147460
  227.8 4.9 %copy-start.9 = (bf16[96,8,8,128]{3,2,1,0:T(8,128)(2,1)S(1)}, bf16[96,8,8,128]{3,2,1,0:T(8,128)(2,1)}, u32[]{:S(2)}) copy-start(bf16[96,8,8,128]{3,2,1,0:T(8,128)(2,1)} %copy-done.8) | copy-start | bytes 4718596
  232.8 3.4 copy-start.7
  236.2 11.9 %copy-start.36 = (f32[768]{0:T(1024)S(1)}, f32[768]{0:T(1024)}, u32[]{:S(2)}) copy-start(f32[768]{0:T(1024)} %fusion.46) | copy-start | bytes 9220
  250.7 3.8 copy-start.35
  256.5 3.2 copy-start.16
  259.3 1.4 copy-start.15
  259.7 2.1 copy-start.20
  261.7 5.6 %copy-start.52 = (bf16[1024,768]{1,0:T(8,128)(2,1)S(1)}, bf16[1024,768]{1,0:T(8,128)(2,1)}, u32[]{:S(2)}) copy-start(bf16[1024,768]{1,0:T(8,128)(2,1)} %param.17) | copy-start | bytes 4718596
  411.4 7.4 %copy-start.14 = (bf16[768,6144]{1,0:T(8,128)(2,1)S(1)}, bf16[768,6144]{1,0:T(8,128)(2,1)}, u32[]{:S(2)}) copy-start(bf16[768,6144]{1,0:T(8,128)(2,1)} %get-tuple-element.26) | copy-start | bytes 28311556
